TPU v7x, 1024 devices: a whole 4x4x32 slice. The times are simulated.
1024 devices in a mesh: dp: 32 (over z_hi, y, core), expert: 32 (over z_lo, x).
Axes of the slice: x: 4, y: 4, z: 32 (z_hi: 4, z_lo: 8; z = z_hi * 8 + z_lo), core: 2. Of those that a mesh axis runs over, the one named last changes fastest.
Arguments:
- tokens: bfloat16 [131072, 2048], P(('dp', 'expert')), may hold values from -6 to 6
- route_ids: int32 [131072, 1], P(('dp', 'expert')), may hold values from 0 to 31; in each aligned block of 128 rows (0 to 127, 128 to 255, ...) at most 5 rows name the same one
- route_gates: float32 [131072, 1], P(('dp', 'expert')), may hold values from 0.2 to 1
- cotangent: bfloat16 [131072, 2048], P(('dp', 'expert')), may hold values from -1.25 to 1.25
- expert_weights: bfloat16 [32, 2048, 1152], P('expert', 'dp'), may hold values from -0.15625 to 0.15625
- master: float32 [32, 2048, 384], P('expert', 'dp'), may hold values from -0.75 to 0.75
- first_moment: float32 [32, 2048, 384], P('expert', 'dp'), may hold values from -6 to 6
- second_moment: float32 [32, 2048, 384], P('expert', 'dp'), may hold values from 0.1 to 2
- old_place: int32 [32], replicated, may hold values from 0 to 31, as said below
- new_place: int32 [32], replicated, may hold values from 0 to 31, as said below
Outputs:
- combined: bfloat16 [131072, 2048], P(('dp', 'expert'))
- gate_grads: float32 [131072, 1], P(('dp', 'expert'))
- expert_grads: float32 [32, 2048, 384], P('expert', 'dp')
- new_master: float32 [32, 2048, 384], P('expert', 'dp')
- new_first: float32 [32, 2048, 384], P('expert', 'dp')
- new_second: float32 [32, 2048, 384], P('expert', 'dp')
Inputs may be any that keep to these rules, and one draw needn't show every extreme that they name: `route_ids`: in the rows of one device (aligned blocks of 128 rows) no expert is named more than 5 times, a bound that some block reaches. `old_place`: A permutation of the experts. `new_place`: A permutation of the experts that differs from old_place in exactly 8 entries.
All inputs are finite; a program needn't handle non-finite values.
Results may differ from a plain program's by a relative error of at most 0.018.
Values may be sent and summed in bfloat16 or wider, within the bound.
A program may use at most 32 MiB of HBM per device.

v0:
```python
import jax
import jax.numpy as jnp
from jax import lax
from jax.sharding import PartitionSpec as P

beta_first = 0.9
beta_second = 0.999
learn_rate = 0.01
adam_eps = 1e-08


def as_sent(value):
    return jax.tree.map(lambda a: a.astype(jnp.bfloat16) if a.dtype == jnp.float32 else a, value)


def silu_value(values):
    return values * jax.nn.sigmoid(values)


def contract_rows(left, right):
    return lax.dot_general(
        left, right, (((0,), (0,)), ((), ())), preferred_element_type=jnp.float32
    )


def shards(
    tokens,
    route_ids,
    route_gates,
    cotangent,
    expert_weights,
    master,
    first_moment,
    second_moment,
    old_place,
    new_place,
):
    experts = lax.axis_size("expert")
    tok_rows = tokens.shape[0]
    routes = route_ids.shape[1]
    capacity = 5 * tok_rows * routes // (4 * experts)
    slots = experts * capacity
    ff_width = expert_weights.shape[2] // 3
    expert_range = jnp.arange(experts, dtype=jnp.int32)
    holder = jnp.sum(
        expert_range[None, :] * (old_place[None, :] == expert_range[:, None]).astype(jnp.int32),
        axis=1,
    )
    flat_ids = route_ids.reshape(-1)
    onehot = (flat_ids[:, None] == expert_range[None, :]).astype(jnp.int32)
    rank_in = jnp.sum((jnp.cumsum(onehot, axis=0) - onehot) * onehot, axis=1)
    target = jnp.sum(onehot * holder[None, :], axis=1)
    slot_index = target * capacity + rank_in
    slot_range = jnp.arange(slots, dtype=jnp.int32)
    place_pairs = (slot_range[:, None] == slot_index[None, :]).astype(jnp.bfloat16)
    place_tokens = jnp.sum(place_pairs.reshape(slots, tok_rows, routes), axis=2)
    send_in = jnp.dot(place_tokens, tokens, preferred_element_type=jnp.float32).astype(jnp.bfloat16)
    scaled = (route_gates[:, :, None] * cotangent[:, None, :].astype(jnp.float32)).astype(
        jnp.bfloat16
    )
    send_up = jnp.dot(
        place_pairs, scaled.reshape(tok_rows * routes, -1), preferred_element_type=jnp.float32
    ).astype(jnp.bfloat16)
    recv_in = lax.all_to_all(send_in, "expert", split_axis=0, concat_axis=0, tiled=True)
    recv_up = lax.all_to_all(send_up, "expert", split_axis=0, concat_axis=0, tiled=True)
    weight_part = expert_weights[0]
    weight = lax.all_gather(weight_part, "dp", axis=0, tiled=True)
    gate_val = jnp.dot(recv_in, weight[:, :ff_width], preferred_element_type=jnp.float32)
    up_val = jnp.dot(
        recv_in, weight[:, ff_width : 2 * ff_width], preferred_element_type=jnp.float32
    )
    hidden = (silu_value(gate_val) * up_val).astype(jnp.bfloat16)
    outputs = lax.dot_general(
        hidden,
        weight[:, 2 * ff_width :],
        (((1,), (1,)), ((), ())),
        preferred_element_type=jnp.float32,
    ).astype(jnp.bfloat16)
    returned = lax.all_to_all(outputs, "expert", split_axis=0, concat_axis=0, tiled=True)
    picked = (
        jnp.take(returned, slot_index, axis=0).reshape(tok_rows, routes, -1).astype(jnp.float32)
    )
    combined = jnp.sum(route_gates[:, :, None] * picked, axis=1).astype(jnp.bfloat16)
    gate_grads = jnp.sum(cotangent[:, None, :].astype(jnp.float32) * picked, axis=2)
    grads = lax.psum_scatter(
        contract_rows(recv_up, hidden)
        .astype(jnp.bfloat16)
        .astype(jnp.float32)
        .astype(jnp.bfloat16),
        "dp",
        scatter_dimension=0,
        tiled=True,
    ).astype(jnp.float32)
    grads = grads[None]
    first = beta_first * first_moment + (1.0 - beta_first) * grads
    second = beta_second * second_moment + (1.0 - beta_second) * grads * grads
    updated = master - learn_rate * first / (jnp.sqrt(second) + adam_eps)
    source_slot = jnp.sum(
        expert_range[None, :] * (old_place[None, :] == new_place[:, None]).astype(jnp.int32), axis=1
    )
    spread = (
        lax.all_to_all(
            updated.astype(jnp.bfloat16), "expert", split_axis=2, concat_axis=0, tiled=True
        ).astype(updated.dtype),
        lax.all_to_all(
            first.astype(jnp.bfloat16), "expert", split_axis=2, concat_axis=0, tiled=True
        ).astype(first.dtype),
        lax.all_to_all(
            second.astype(jnp.bfloat16), "expert", split_axis=2, concat_axis=0, tiled=True
        ).astype(second.dtype),
    )
    ordered = tuple((jnp.take(piece, source_slot, axis=0) for piece in spread))
    new_master, new_first, new_second = jax.tree.map(
        lambda part, own: part.astype(own.dtype),
        lax.all_to_all(as_sent(ordered), "expert", split_axis=0, concat_axis=2, tiled=True),
        ordered,
    )
    return (combined, gate_grads, grads, new_master, new_first, new_second)


def solution(mesh):
    in_specs = (
        P(("dp", "expert"), None),
        P(("dp", "expert"), None),
        P(("dp", "expert"), None),
        P(("dp", "expert"), None),
        P("expert", "dp", None),
        P("expert", "dp", None),
        P("expert", "dp", None),
        P("expert", "dp", None),
        P(),
        P(),
    )
    out_specs = (
        P(("dp", "expert"), None),
        P(("dp", "expert"), None),
        P("expert", "dp", None),
        P("expert", "dp", None),
        P("expert", "dp", None),
        P("expert", "dp", None),
    )
    return jax.shard_map(shards, mesh=mesh, in_specs=in_specs, out_specs=out_specs, check_vma=False)
```

profile of v0, /device:TPU:24, one launch (start us, length us, event | category | flops | bytes accessed | tf_op | source)
XLA Modules:
  0.0 581.5 jit_solution(9776933983339483302)
XLA Ops:
  7.2 0.8 fusion.20
  8.0 0.9 select_reduce_fusion.2
  8.8 0.2 reduce_window_sum.11
  9.0 0.8 select_reduce_fusion.1
  9.9 0.3 convolution_convert_fusion.3
  10.2 1.3 all_to_all.66
  11.5 15.4 %all-to-all-start = ((bf16[32,5,2048]{2,1,0:T(8,128)(2,1)}), bf16[32,5,2048]{2,1,0:T(8,128)(2,1)S(1)}, u32[]{:S(2)}, u32[]{:S(2)}) async-start(bf16[32,5,2048]{2,1,0:T(8,128)(2,1)} %all_to_all.66), calls=%async_computation | async-start | bytes 2097152 | tf_op jit(solution)/shard_map/all_to_all | solution.py:64
  26.9 0.7 all-gather.3.cloned.1.call-update
  27.6 0.4 convolution_convert_fusion.1
  28.1 1.3 all_to_all.72
  29.3 56.4 %all-to-all-done = bf16[32,5,2048]{2,1,0:T(8,128)(2,1)S(1)} async-done(((bf16[32,5,2048]{2,1,0:T(8,128)(2,1)}), bf16[32,5,2048]{2,1,0:T(8,128)(2,1)S(1)}, u32[]{:S(2)}, u32[]{:S(2)}) %all-to-all-start) | async-done | bytes 655392 | tf_op jit(solution)/shard_map/all_to_all | solution.py:64
  85.7 10.6 %all-to-all-start.2 = ((bf16[32,5,2048]{2,1,0:T(8,128)(2,1)}), bf16[32,5,2048]{2,1,0:T(8,128)(2,1)S(1)}, u32[]{:S(2)}, u32[]{:S(2)}) async-start(bf16[32,5,2048]{2,1,0:T(8,128)(2,1)} %all_to_all.72), calls=%async_computation.2 | async-start | bytes 2097152 | tf_op jit(solution)/shard_map/all_to_all | solution.py:65
  96.3 1.1 all_to_all.68
  97.4 107.9 %all-to-all-done.2 = bf16[32,5,2048]{2,1,0:T(8,128)(2,1)S(1)} async-done(((bf16[32,5,2048]{2,1,0:T(8,128)(2,1)}), bf16[32,5,2048]{2,1,0:T(8,128)(2,1)S(1)}, u32[]{:S(2)}, u32[]{:S(2)}) %all-to-all-start.2) | async-done | bytes 655392 | tf_op jit(solution)/shard_map/all_to_all | solution.py:65
  205.3 0.3 all_to_all.74
  205.6 2.2 fusion.3
  207.8 1.9 fusion.8
  209.8 1.9 convolution_convert_fusion
  211.7 200.3 %reduce-scatter.2.cloned.1.call-done = bf16[64,384]{1,0:T(8,128)(2,1)} async-done(((bf16[2048,384]{1,0:T(8,128)(2,1)}), bf16[64,384]{1,0:T(8,128)(2,1)}) %reduce-scatter.2.cloned.1.call-update) | async-done | bytes 49168 | tf_op jit(solution)/shard_map/reduce_scatter | solution.py:85
  412.0 0.9 fusion.21
  412.9 0.2 copy.38
  413.0 0.5 broadcast.94
  413.6 1.3 reduce.2
  414.8 0.8 reshape.230
  415.6 10.7 %all-to-all-start.7 = ((bf16[32,2,384]{2,1,0:T(2,128)(2,1)}), bf16[32,2,384]{2,1,0:T(2,128)(2,1)S(1)}, u32[]{:S(2)}, u32[]{:S(2)}) async-start(bf16[32,2,384]{2,1,0:T(2,128)(2,1)} %reshape.230), calls=%async_computation.8 | async-start | bytes 98304 | tf_op jit(solution)/shard_map/all_to_all | solution.py:108
  426.3 0.2 copy.36
  426.5 1.3 reduce.3
  427.8 0.8 reshape.226
  428.5 10.6 %all-to-all-done.7 = bf16[32,2,384]{2,1,0:T(2,128)(2,1)S(1)} async-done(((bf16[32,2,384]{2,1,0:T(2,128)(2,1)}), bf16[32,2,384]{2,1,0:T(2,128)(2,1)S(1)}, u32[]{:S(2)}, u32[]{:S(2)}) %all-to-all-start.7) | async-done | bytes 49184 | tf_op jit(solution)/shard_map/all_to_all | solution.py:108
  439.1 3.9 all-to-all-start.5
  442.9 0.2 copy.34
  443.1 1.3 reduce.4
  444.4 0.8 reshape.222
  445.2 10.6 %all-to-all-done.5 = bf16[32,2,384]{2,1,0:T(2,128)(2,1)S(1)} async-done(((bf16[32,2,384]{2,1,0:T(2,128)(2,1)}), bf16[32,2,384]{2,1,0:T(2,128)(2,1)S(1)}, u32[]{:S(2)}, u32[]{:S(2)}) %all-to-all-start.5) | async-done | bytes 49184 | tf_op jit(solution)/shard_map/all_to_all | solution.py:105
  455.7 3.9 all-to-all-start.3
  460.0 0.6 gather_fusion.3
  460.6 0.6 gather_fusion.2
  461.2 11.2 %all-to-all-done.3 = bf16[32,2,384]{2,1,0:T(2,128)(2,1)S(1)} async-done(((bf16[32,2,384]{2,1,0:T(2,128)(2,1)}), bf16[32,2,384]{2,1,0:T(2,128)(2,1)S(1)}, u32[]{:S(2)}, u32[]{:S(2)}) %all-to-all-start.3) | async-done | bytes 49184 | tf_op jit(solution)/shard_map/all_to_all | solution.py:102
  472.5 0.6 gather_fusion.1
  473.1 0.1 select_convert_fusion
  473.3 0.8 reshape.224
  474.0 3.9 all-to-all-start.4
  477.9 0.8 reshape.228
  478.7 12.0 %all-to-all-done.4 = bf16[32,2,384]{2,1,0:T(2,128)(2,1)S(1)} async-done(((bf16[32,2,384]{2,1,0:T(2,128)(2,1)}), bf16[32,2,384]{2,1,0:T(2,128)(2,1)S(1)}, u32[]{:S(2)}, u32[]{:S(2)}) %all-to-all-start.4) | async-done | bytes 49184 | tf_op jit(solution)/shard_map/all_to_all | solution.py:115
  490.7 3.9 all-to-all-start.6
  494.5 0.8 reshape.232
  495.3 12.0 %all-to-all-done.6 = bf16[32,2,384]{2,1,0:T(2,128)(2,1)S(1)} async-done(((bf16[32,2,384]{2,1,0:T(2,128)(2,1)}), bf16[32,2,384]{2,1,0:T(2,128)(2,1)S(1)}, u32[]{:S(2)}, u32[]{:S(2)}) %all-to-all-start.6) | async-done | bytes 49184 | tf_op jit(solution)/shard_map/all_to_all | solution.py:115
  507.3 4.0 all-to-all-start.8
  511.4 2.1 convolution_convert_fusion.2
  513.5 1.2 all_to_all.69
  514.7 9.4 %all-to-all-done.8 = bf16[32,2,384]{2,1,0:T(2,128)(2,1)S(1)} async-done(((bf16[32,2,384]{2,1,0:T(2,128)(2,1)}), bf16[32,2,384]{2,1,0:T(2,128)(2,1)S(1)}, u32[]{:S(2)}, u32[]{:S(2)}) %all-to-all-start.8) | async-done | bytes 49184 | tf_op jit(solution)/shard_map/all_to_all | solution.py:115
  524.1 3.9 all-to-all-start.1
  528.0 0.6 convert_bitcast_fusion.3
  528.7 0.1 reshape.225
  528.8 0.2 reshape.169
  529.0 0.8 copy.40
  530.0 0.2 reshape.171
  530.2 0.8 copy.41
  531.1 0.2 reshape.173
  531.3 0.8 copy.42
  532.0 39.8 %all-to-all-done.1 = bf16[32,5,2048]{2,1,0:T(8,128)(2,1)S(1)} async-done(((bf16[32,5,2048]{2,1,0:T(8,128)(2,1)}), bf16[32,5,2048]{2,1,0:T(8,128)(2,1)S(1)}, u32[]{:S(2)}, u32[]{:S(2)}) %all-to-all-start.1) | async-done | bytes 655392 | tf_op jit(solution)/shard_map/all_to_all | solution.py:79
  571.9 0.3 all_to_all.71
  572.1 0.9 gather_fusion
  573.1 1.6 fusion.12
  (37 shorter events, 1.0 us)
Async XLA Ops:
  7.2 2.7 copy-start
  10.2 17.4 %copy-start.1 = (bf16[128,2048]{1,0:T(8,128)(2,1)S(1)}, bf16[128,2048]{1,0:T(8,128)(2,1)}, u32[]{:S(2)}) copy-start(bf16[128,2048]{1,0:T(8,128)(2,1)} %param.15) | copy-start | bytes 1572868
  10.2 17.4 %copy-start.7 = (f32[128,1]{0,1:T(1,128)S(1)}, f32[128,1]{0,1:T(1,128)}, u32[]{:S(2)}) copy-start(f32[128,1]{0,1:T(1,128)} %param.14) | copy-start | bytes 1540
  11.5 74.2 %all-to-all-start = ((bf16[32,5,2048]{2,1,0:T(8,128)(2,1)}), bf16[32,5,2048]{2,1,0:T(8,128)(2,1)S(1)}, u32[]{:S(2)}, u32[]{:S(2)}) async-start(bf16[32,5,2048]{2,1,0:T(8,128)(2,1)} %all_to_all.66), calls=%async_computation | async-start | bytes 2097152 | tf_op jit(solution)/shard_map/all_to_all | solution.py:64
  26.9 178.7 %all-gather.3.cloned.1.call-start = ((), (), s32[]{:S(2)}) async-start(), calls=%async_computation.11 | async-start | bytes 4866048 | tf_op jit(solution)/shard_map/all_gather | solution.py:67
  85.7 119.6 %all-to-all-start.2 = ((bf16[32,5,2048]{2,1,0:T(8,128)(2,1)}), bf16[32,5,2048]{2,1,0:T(8,128)(2,1)S(1)}, u32[]{:S(2)}, u32[]{:S(2)}) async-start(bf16[32,5,2048]{2,1,0:T(8,128)(2,1)} %all_to_all.72), calls=%async_computation.2 | async-start | bytes 2097152 | tf_op jit(solution)/shard_map/all_to_all | solution.py:65
  96.3 315.7 %reduce-scatter.2.cloned.1.call-start = ((), (), s32[]{:S(2)}) async-start(), calls=%async_computation.10 | async-start | bytes 1622016 | tf_op jit(solution)/shard_map/reduce_scatter | solution.py:85
  205.6 2.2 copy-start.2
  209.7 202.2 %copy-start.4 = (f32[1,64,384]{2,1,0:T(8,128)S(1)}, f32[1,64,384]{2,1,0:T(8,128)}, u32[]{:S(2)}) copy-start(f32[1,64,384]{2,1,0:T(8,128)} %param.19) | copy-start | bytes 294916
  209.7 202.2 %copy-start.5 = (f32[1,64,384]{2,1,0:T(8,128)S(1)}, f32[1,64,384]{2,1,0:T(8,128)}, u32[]{:S(2)}) copy-start(f32[1,64,384]{2,1,0:T(8,128)} %param.17) | copy-start | bytes 294916
  209.8 202.2 %copy-start.6 = (f32[1,64,384]{2,1,0:T(8,128)S(1)}, f32[1,64,384]{2,1,0:T(8,128)}, u32[]{:S(2)}) copy-start(f32[1,64,384]{2,1,0:T(8,128)} %param.18) | copy-start | bytes 294916
  415.6 23.5 %all-to-all-start.7 = ((bf16[32,2,384]{2,1,0:T(2,128)(2,1)}), bf16[32,2,384]{2,1,0:T(2,128)(2,1)S(1)}, u32[]{:S(2)}, u32[]{:S(2)}) async-start(bf16[32,2,384]{2,1,0:T(2,128)(2,1)} %reshape.230), calls=%async_computation.8 | async-start | bytes 98304 | tf_op jit(solution)/shard_map/all_to_all | solution.py:108
  439.1 16.6 %all-to-all-start.5 = ((bf16[32,2,384]{2,1,0:T(2,128)(2,1)}), bf16[32,2,384]{2,1,0:T(2,128)(2,1)S(1)}, u32[]{:S(2)}, u32[]{:S(2)}) async-start(bf16[32,2,384]{2,1,0:T(2,128)(2,1)} %reshape.226), calls=%async_computation.6 | async-start | bytes 98304 | tf_op jit(solution)/shard_map/all_to_all | solution.py:105
  455.7 16.6 %all-to-all-start.3 = ((bf16[32,2,384]{2,1,0:T(2,128)(2,1)}), bf16[32,2,384]{2,1,0:T(2,128)(2,1)S(1)}, u32[]{:S(2)}, u32[]{:S(2)}) async-start(bf16[32,2,384]{2,1,0:T(2,128)(2,1)} %reshape.222), calls=%async_computation.4 | async-start | bytes 98304 | tf_op jit(solution)/shard_map/all_to_all | solution.py:102
  474.0 16.6 %all-to-all-start.4 = ((bf16[32,2,384]{2,1,0:T(2,128)(2,1)}), bf16[32,2,384]{2,1,0:T(2,128)(2,1)S(1)}, u32[]{:S(2)}, u32[]{:S(2)}) async-start(bf16[32,2,384]{2,1,0:T(2,128)(2,1)} %reshape.224), calls=%async_computation.5 | async-start | bytes 98304 | tf_op jit(solution)/shard_map/all_to_all | solution.py:115
  490.7 16.6 %all-to-all-start.6 = ((bf16[32,2,384]{2,1,0:T(2,128)(2,1)}), bf16[32,2,384]{2,1,0:T(2,128)(2,1)S(1)}, u32[]{:S(2)}, u32[]{:S(2)}) async-start(bf16[32,2,384]{2,1,0:T(2,128)(2,1)} %reshape.228), calls=%async_computation.7 | async-start | bytes 98304 | tf_op jit(solution)/shard_map/all_to_all | solution.py:115
  507.3 16.7 %all-to-all-start.8 = ((bf16[32,2,384]{2,1,0:T(2,128)(2,1)}), bf16[32,2,384]{2,1,0:T(2,128)(2,1)S(1)}, u32[]{:S(2)}, u32[]{:S(2)}) async-start(bf16[32,2,384]{2,1,0:T(2,128)(2,1)} %reshape.232), calls=%async_computation.9 | async-start | bytes 98304 | tf_op jit(solution)/shard_map/all_to_all | solution.py:115
  513.4 14.6 %copy-start.3 = (bf16[64,384]{1,0:T(8,128)(2,1)S(1)}, bf16[64,384]{1,0:T(8,128)(2,1)}, u32[]{:S(2)}) copy-start(bf16[64,384]{1,0:T(8,128)(2,1)} %reduce-scatter.2.cloned.1.call-done) | copy-start | bytes 147460
  524.1 47.8 %all-to-all-start.1 = ((bf16[32,5,2048]{2,1,0:T(8,128)(2,1)}), bf16[32,5,2048]{2,1,0:T(8,128)(2,1)S(1)}, u32[]{:S(2)}, u32[]{:S(2)}) async-start(bf16[32,5,2048]{2,1,0:T(8,128)(2,1)} %all_to_all.69), calls=%async_computation.1 | async-start | bytes 2097152 | tf_op jit(solution)/shard_map/all_to_all | solution.py:79
Sparse Core Ops, SparseCore 0:
  32.0 150.3 all-gather.2
  211.8 200.0 reduce-scatter.1
where the time goes:
time: 582 us
  waiting for transfers between devices  471 us (81%)
  starting transfers between devices  60.1 us (10%)
  local copies, waits for them, and re-layouts  17.4 us (3%)
  between operations  14.5 us (2%)
  other arithmetic  9.85 us (2%)
  matrix products  8.83 us (2%)
    reduce_scatter x1, waiting for transfers between devices, shards(): lax.psum_scatter(contract_rows(recv_up, hidden).astype(jnp.bfloat16).asty...  200 us
    all_to_all x1, waiting for transfers between devices, shards(): lax.all_to_all(send_up, 'expert', split_axis=0, concat_axis=0, tiled=True)  108 us
    all_to_all x1, waiting for transfers between devices, shards(): lax.all_to_all(send_in, 'expert', split_axis=0, concat_axis=0, tiled=True)  56.4 us
    all_to_all x1, waiting for transfers between devices, shards(): lax.all_to_all(outputs, 'expert', split_axis=0, concat_axis=0, tiled=True)  39.8 us
    all_to_all x3, waiting for transfers between devices, shards(): lax.all_to_all(as_sent(ordered), 'expert', split_axis=0, concat_axis=2, t...  33.4 us
    all_to_all x1, starting transfers between devices, shards(): lax.all_to_all(send_in, 'expert', split_axis=0, concat_axis=0, tiled=True)  15.4 us
    all_to_all x3, starting transfers between devices, shards(): lax.all_to_all(as_sent(ordered), 'expert', split_axis=0, concat_axis=2, t...  11.7 us
  transfers between devices with their start and end apart: 11, of which 10 were waited for; matrix products, arithmetic and copies ran while one was open for 2% of the time, Pallas kernels for 0%

commit v1 on v0

v1 whole, which is shorter than its diff:
```python
import functools

import jax
import jax.numpy as jnp
from jax import lax
from jax.experimental import pallas as pl
from jax.experimental.pallas import tpu as pltpu
from jax.sharding import PartitionSpec as P

beta_first = 0.9
beta_second = 0.999
learn_rate = 0.01
adam_eps = 1e-08

MESH = pl.DeviceIdType.MESH
ANY = pl.BlockSpec(memory_space=pl.ANY)
VMEM = pl.BlockSpec(memory_space=pltpu.VMEM)
RING = 4
CORES = 2


def silu_value(values):
    return values * jax.nn.sigmoid(values)


def contract_rows(left, right):
    return lax.dot_general(
        left, right, (((0,), (0,)), ((), ())), preferred_element_type=jnp.float32
    )


def place():
    dp, ex = lax.axis_index("dp"), lax.axis_index("expert")
    return dp, ex, dp // (RING * CORES), (dp // CORES) % RING, dp % CORES


def index_of(z, y, core):
    return ((z % RING) * RING + y % RING) * CORES + core


def send(src, dst, send_sem, recv_sem, device):
    return pltpu.make_async_remote_copy(
        src_ref=src,
        dst_ref=dst,
        send_sem=send_sem,
        recv_sem=recv_sem,
        device_id=device,
        device_id_type=MESH,
    )


def greet(devices, experts, dp, ex):
    barrier = pltpu.get_barrier_semaphore()
    for device in devices:
        pl.semaphore_signal(barrier, inc=1, device_id=device, device_id_type=MESH)

    def one(step, carry):
        pl.semaphore_signal(
            barrier, inc=1, device_id=(dp, (ex + step) % experts), device_id_type=MESH
        )
        return carry

    lax.fori_loop(1, experts, one, 0)
    pl.semaphore_wait(barrier, len(devices) + experts - 1)


def exchange(experts, dp, ex, src, dst, send_sems, recv_sems):
    def copy(step):
        target = (ex + step) % experts
        return send(
            src.at[target], dst.at[ex], send_sems.at[target], recv_sems.at[ex], (dp, target)
        )

    def start(step, carry):
        copy(step).start()
        return carry

    def finish(step, carry):
        other = (ex + step) % experts
        send(
            src.at[other], dst.at[other], send_sems.at[other], recv_sems.at[other], (dp, other)
        ).wait()
        return carry

    lax.fori_loop(1, experts, start, 0)
    return lambda: lax.fori_loop(1, experts, finish, 0)


def dispatch_kernel(
    experts,
    weight_ref,
    in_ref,
    up_ref,
    whole_ref,
    recv_in_ref,
    recv_up_ref,
    local_sems,
    in_send,
    in_recv,
    up_send,
    up_recv,
    z_send,
    z_recv,
    y_send,
    y_recv,
    c_send,
    c_recv,
):
    dp, ex, z, y, core = place()
    half = weight_ref.shape[0] // 2
    right, left = (index_of(z + 1, y, core), ex), (index_of(z + 3, y, core), ex)
    sibling = (index_of(z, y, 1 - core), ex)
    ring_y = [(index_of(z, y + s, core), ex) for s in range(1, RING)]
    greet([right, left, sibling] + ring_y, experts, dp, ex)

    own = [
        pltpu.make_async_copy(weight_ref, whole_ref.at[dp], local_sems.at[0]),
        pltpu.make_async_copy(in_ref.at[ex], recv_in_ref.at[ex], local_sems.at[1]),
        pltpu.make_async_copy(up_ref.at[ex], recv_up_ref.at[ex], local_sems.at[2]),
    ]
    for copy in own:
        copy.start()

    sent = []

    def start(copy):
        copy.start()
        sent.append(copy)

    blocks = [dp, left[0], right[0], index_of(z + 2, y, core)]
    low, high = pl.ds(0, half), pl.ds(half, half)

    def z_copy(i, src, index, part, device):
        return send(src, whole_ref.at[index, part], z_send.at[i], z_recv.at[i], device)

    def z_arrival(i, index, part):
        there = whole_ref.at[index, part]
        return send(there, there, z_send.at[i], z_recv.at[i], right)

    whole = pl.ds(0, 2 * half)
    start(z_copy(0, weight_ref, dp, whole, right))
    start(z_copy(1, weight_ref, dp, whole, left))

    def spread(k, src):
        for s in range(1, RING):
            start(
                send(
                    src,
                    whole_ref.at[blocks[k]],
                    y_send.at[k, s - 1],
                    y_recv.at[k, s - 1],
                    ring_y[s - 1],
                )
            )
        start(send(src, whole_ref.at[blocks[k]], c_send.at[k, 0], c_recv.at[k, 0], sibling))

    def pass_on(k):
        for s in range(1, RING):
            index = index_of(blocks[k] // (RING * CORES), y + RING - s, core)
            there = whole_ref.at[index]
            send(there, there, y_send.at[k, s - 1], y_recv.at[k, s - 1], sibling).wait_recv()
            start(send(there, there, c_send.at[k, s], c_recv.at[k, s], sibling))

    spread(0, weight_ref)
    finish_in = exchange(experts, dp, ex, in_ref, recv_in_ref, in_send, in_recv)
    finish_up = exchange(experts, dp, ex, up_ref, recv_up_ref, up_send, up_recv)
    z_arrival(0, blocks[1], whole).wait_recv()
    start(z_copy(2, whole_ref.at[blocks[1], low], blocks[1], low, right))
    spread(1, whole_ref.at[blocks[1]])
    z_arrival(1, blocks[2], whole).wait_recv()
    start(z_copy(3, whole_ref.at[blocks[2], high], blocks[2], high, left))
    spread(2, whole_ref.at[blocks[2]])
    pass_on(0)
    z_arrival(2, blocks[3], low).wait_recv()
    z_arrival(3, blocks[3], high).wait_recv()
    spread(3, whole_ref.at[blocks[3]])
    pass_on(1)
    pass_on(2)
    pass_on(3)
    for k in range(RING):
        for s in range(RING):
            index = index_of(blocks[k] // (RING * CORES), y + RING - s, 1 - core)
            there = whole_ref.at[index]
            send(there, there, c_send.at[k, s], c_recv.at[k, s], sibling).wait_recv()
    for copy in sent:
        copy.wait_send()
    finish_in()
    finish_up()
    for copy in own:
        copy.wait()


def dispatch(weight, send_in, send_up, devices):
    experts = send_in.shape[0]
    dma = pltpu.SemaphoreType.DMA
    return pl.pallas_call(
        functools.partial(dispatch_kernel, experts),
        out_shape=[
            jax.ShapeDtypeStruct((devices,) + weight.shape, weight.dtype),
            jax.ShapeDtypeStruct(send_in.shape, send_in.dtype),
            jax.ShapeDtypeStruct(send_up.shape, send_up.dtype),
        ],
        in_specs=[ANY] * 3,
        out_specs=[ANY] * 3,
        scratch_shapes=[dma((3,))]
        + [dma((experts,))] * 4
        + [dma((RING,))] * 2
        + [dma((RING, RING - 1))] * 2
        + [dma((RING, RING))] * 2,
        compiler_params=pltpu.CompilerParams(collective_id=0, has_side_effects=True),
        name="dispatch",
    )(weight, send_in, send_up)


def give_back_kernel(
    experts,
    out_ref,
    partial_ref,
    returned_ref,
    grads_ref,
    c_buf,
    y_from,
    y_buf,
    z_from,
    z_buf,
    local_sem,
    out_send,
    out_recv,
    c_send,
    c_recv,
    y_send,
    y_recv,
    z_send,
    z_recv,
):
    dp, ex, z, y, core = place()
    sibling = (index_of(z, y, 1 - core), ex)
    ring_y = [(index_of(z, y + s, core), ex) for s in range(1, RING)]
    ring_z = [(index_of(z + s, y, core), ex) for s in range(1, RING)]
    greet([sibling] + ring_y + ring_z, experts, dp, ex)

    to_core = send(partial_ref.at[:, :, 1 - core], c_buf, c_send, c_recv, sibling)
    to_core.start()
    own = pltpu.make_async_copy(out_ref.at[ex], returned_ref.at[ex], local_sem)
    own.start()
    finish_out = exchange(experts, dp, ex, out_ref, returned_ref, out_send, out_recv)
    to_core.wait()

    def pair(i, carry):
        at, row = i // RING, i % RING
        y_from[row, at] = (
            partial_ref[at, row, core].astype(jnp.float32) + c_buf[at, row].astype(jnp.float32)
        ).astype(y_from.dtype)
        return carry

    lax.fori_loop(0, RING * RING, pair, 0)
    y_copies = [
        send(
            y_from.at[(y + s) % RING],
            y_buf.at[s - 1],
            y_send.at[s - 1],
            y_recv.at[s - 1],
            ring_y[s - 1],
        )
        for s in range(1, RING)
    ]
    for copy in y_copies:
        copy.start()
    for copy in y_copies:
        copy.wait()

    def quad(i, carry):
        total = y_from[y, i].astype(jnp.float32)
        for s in range(RING - 1):
            total += y_buf[s, i].astype(jnp.float32)
        z_from[i] = total.astype(z_from.dtype)
        return carry

    lax.fori_loop(0, RING, quad, 0)
    z_copies = [
        send(
            z_from.at[(z + s) % RING],
            z_buf.at[s - 1],
            z_send.at[s - 1],
            z_recv.at[s - 1],
            ring_z[s - 1],
        )
        for s in range(1, RING)
    ]
    for copy in z_copies:
        copy.start()
    for copy in z_copies:
        copy.wait()
    total = z_from[z].astype(jnp.float32)
    for s in range(RING - 1):
        total += z_buf[s].astype(jnp.float32)
    grads_ref[...] = total
    finish_out()
    own.wait()


def give_back(outputs, partial):
    experts = outputs.shape[0]
    dma = pltpu.SemaphoreType.DMA
    rows, width = partial.shape[3:]
    block = (rows, width)
    return pl.pallas_call(
        functools.partial(give_back_kernel, experts),
        out_shape=[
            jax.ShapeDtypeStruct(outputs.shape, outputs.dtype),
            jax.ShapeDtypeStruct(block, jnp.float32),
        ],
        in_specs=[ANY, VMEM],
        out_specs=[ANY, VMEM],
        scratch_shapes=[
            pltpu.VMEM((RING, RING) + block, partial.dtype),
            pltpu.VMEM((RING, RING) + block, partial.dtype),
            pltpu.VMEM((RING - 1, RING) + block, partial.dtype),
            pltpu.VMEM((RING,) + block, partial.dtype),
            pltpu.VMEM((RING - 1,) + block, partial.dtype),
            dma,
            dma((experts,)),
            dma((experts,)),
            dma,
            dma,
        ]
        + [dma((RING - 1,))] * 4,
        compiler_params=pltpu.CompilerParams(
            collective_id=1, has_side_effects=True, vmem_limit_bytes=24 * 1024 * 1024
        ),
        name="give_back",
    )(outputs, partial)


def shards(
    tokens,
    route_ids,
    route_gates,
    cotangent,
    expert_weights,
    master,
    first_moment,
    second_moment,
    old_place,
    new_place,
):
    experts = lax.axis_size("expert")
    devices = lax.axis_size("dp")
    tok_rows, model = tokens.shape
    routes = route_ids.shape[1]
    capacity = 5 * tok_rows * routes // (4 * experts)
    slots = experts * capacity
    ff_width = expert_weights.shape[2] // 3
    expert_range = jnp.arange(experts, dtype=jnp.int32)
    holder = jnp.sum(
        expert_range[None, :] * (old_place[None, :] == expert_range[:, None]).astype(jnp.int32),
        axis=1,
    )
    flat_ids = route_ids.reshape(-1)
    onehot = (flat_ids[:, None] == expert_range[None, :]).astype(jnp.int32)
    rank_in = jnp.sum((jnp.cumsum(onehot, axis=0) - onehot) * onehot, axis=1)
    target = jnp.sum(onehot * holder[None, :], axis=1)
    slot_index = target * capacity + rank_in
    slot_range = jnp.arange(slots, dtype=jnp.int32)
    place_pairs = (slot_range[:, None] == slot_index[None, :]).astype(jnp.bfloat16)
    place_tokens = jnp.sum(place_pairs.reshape(slots, tok_rows, routes), axis=2)
    send_in = jnp.dot(place_tokens, tokens, preferred_element_type=jnp.float32).astype(jnp.bfloat16)
    scaled = (route_gates[:, :, None] * cotangent[:, None, :].astype(jnp.float32)).astype(
        jnp.bfloat16
    )
    send_up = jnp.dot(
        place_pairs, scaled.reshape(tok_rows * routes, -1), preferred_element_type=jnp.float32
    ).astype(jnp.bfloat16)
    packed = (experts, capacity * model // 128, 128)
    weight, recv_in, recv_up = dispatch(
        expert_weights[0], send_in.reshape(packed), send_up.reshape(packed), devices
    )
    weight = weight.reshape(model, -1)
    recv_in = recv_in.reshape(slots, model)
    recv_up = recv_up.reshape(slots, model)
    gate_val = jnp.dot(recv_in, weight[:, :ff_width], preferred_element_type=jnp.float32)
    up_val = jnp.dot(
        recv_in, weight[:, ff_width : 2 * ff_width], preferred_element_type=jnp.float32
    )
    hidden = (silu_value(gate_val) * up_val).astype(jnp.bfloat16)
    outputs = lax.dot_general(
        hidden,
        weight[:, 2 * ff_width :],
        (((1,), (1,)), ((), ())),
        preferred_element_type=jnp.float32,
    ).astype(jnp.bfloat16)
    partial = contract_rows(recv_up, hidden).astype(jnp.bfloat16)
    returned, grads = give_back(
        outputs.reshape(packed), partial.reshape(RING, RING, CORES, -1, ff_width)
    )
    returned = returned.reshape(slots, model)
    picked = (
        jnp.take(returned, slot_index, axis=0).reshape(tok_rows, routes, -1).astype(jnp.float32)
    )
    combined = jnp.sum(route_gates[:, :, None] * picked, axis=1).astype(jnp.bfloat16)
    gate_grads = jnp.sum(cotangent[:, None, :].astype(jnp.float32) * picked, axis=2)
    grads = grads[None]
    first = beta_first * first_moment + (1.0 - beta_first) * grads
    second = beta_second * second_moment + (1.0 - beta_second) * grads * grads
    updated = master - learn_rate * first / (jnp.sqrt(second) + adam_eps)
    source_slot = jnp.sum(
        expert_range[None, :] * (old_place[None, :] == new_place[:, None]).astype(jnp.int32), axis=1
    )
    state = jnp.concatenate([updated, first, second], axis=2).astype(jnp.bfloat16)
    rows = state.shape[1]
    state = state.reshape(experts, rows // experts, -1)
    spread = lax.all_to_all(state, "expert", split_axis=0, concat_axis=0, tiled=True)
    ordered = jnp.take(spread, source_slot, axis=0)
    moved = lax.all_to_all(ordered, "expert", split_axis=0, concat_axis=0, tiled=True)
    moved = moved.reshape(1, rows, 3, ff_width).astype(jnp.float32)
    return (combined, gate_grads, grads, moved[:, :, 0], moved[:, :, 1], moved[:, :, 2])


def solution(mesh):
    in_specs = (
        P(("dp", "expert"), None),
        P(("dp", "expert"), None),
        P(("dp", "expert"), None),
        P(("dp", "expert"), None),
        P("expert", "dp", None),
        P("expert", "dp", None),
        P("expert", "dp", None),
        P("expert", "dp", None),
        P(),
        P(),
    )
    out_specs = (
        P(("dp", "expert"), None),
        P(("dp", "expert"), None),
        P("expert", "dp", None),
        P("expert", "dp", None),
        P("expert", "dp", None),
        P("expert", "dp", None),
    )
    return jax.shard_map(shards, mesh=mesh, in_specs=in_specs, out_specs=out_specs, check_vma=False)
```

time: 582 us -> 262 us (0.45)
  waiting for transfers between devices: 471 us -> 23.7 us
  Pallas kernels: 0 us -> 175 us
  starting transfers between devices: 60.1 us -> 36.5 us
  between operations: 14.5 us -> 0.93 us
  local copies, waits for them, and re-layouts: 17.4 us -> 9.49 us
    all_to_all x9 -> x2, waiting for transfers between devices: 270 us -> 23.7 us  [the longest x1 13.3 us: shards(): lax.all_to_all(state, 'expert', split_axis=0, concat_axis=0, tiled=True)]
    reduce_scatter x1 -> x0, waiting for transfers between devices: 200 us -> none  [shards(): lax.psum_scatter(contract_rows(recv_up, hidden).astype(jnp.bfloat16).asty...]
    pallas_call x0 -> x2, Pallas kernels: none -> 175 us  [the longest x1 108 us: dispatch(): pl.pallas_call(functools.partial(dispatch_kernel, experts), out_shape=[ja...]
    all_to_all x9 -> x2, starting transfers between devices: 60 us -> 36.5 us  [the longest x1 31.7 us: shards(): lax.all_to_all(state, 'expert', split_axis=0, concat_axis=0, tiled=True)]
  transfers between devices with their start and end apart: 11 -> 2, of which waited for: 10 -> 2; matrix products, arithmetic and copies ran while one was open for 2% -> 1% of each run, Pallas kernels for 0% -> 0%
where the time goes in v1:
time: 262 us; the launch traced here: 260 us
  Pallas kernels  175 us (67%)
  starting transfers between devices  36.5 us (14%)
  waiting for transfers between devices  23.7 us (9%)
  local copies, waits for them, and re-layouts  9.49 us (4%)
  matrix products  8.47 us (3%)
  other arithmetic  6.03 us (2%)
    pallas_call x1, Pallas kernels, dispatch(): pl.pallas_call(functools.partial(dispatch_kernel, experts), out_shape=[ja...  108 us
    pallas_call x1, Pallas kernels, give_back(): pl.pallas_call(functools.partial(give_back_kernel, experts), out_shape=[j...  66.5 us
    all_to_all x1, starting transfers between devices, shards(): lax.all_to_all(state, 'expert', split_axis=0, concat_axis=0, tiled=True)  31.7 us
    all_to_all x1, waiting for transfers between devices, shards(): lax.all_to_all(state, 'expert', split_axis=0, concat_axis=0, tiled=True)  13.3 us
    all_to_all x1, waiting for transfers between devices, shards(): lax.all_to_all(ordered, 'expert', split_axis=0, concat_axis=0, tiled=True)  10.4 us
  transfers between devices with their start and end apart: 2, of which 2 were waited for; matrix products, arithmetic and copies ran while one was open for 1% of the time, Pallas kernels for 0%

profile of v1, /device:TPU:24, one launch (start us, length us, event | category | flops | bytes accessed | tf_op | source)
XLA Modules:
  0.0 259.9 jit_solution(7128011479580038710)
XLA Ops:
  0.6 0.0 copy-start
  0.6 0.8 fusion.18
  1.4 0.2 reduce_window_sum.11
  1.6 0.8 select_reduce_fusion.2
  2.5 0.8 select_reduce_fusion.1
  3.3 1.4 convolution_convert_fusion.2
  4.8 1.2 reshape.175.up_ref
  6.0 0.0 copy-done
  6.0 0.3 convolution_convert_fusion.3
  6.3 1.1 reshape.174.in_ref
  7.4 108.2 %dispatch.1 = (bf16[32,64,1152]{2,1,0:T(8,128)(2,1)}, bf16[32,80,128]{2,1,0:T(8,128)(2,1)}, bf16[32,80,128]{2,1,0:T(8,128)(2,1)}) custom-call(bf16[64,1152]{1,0:T(8,128)(2,1)} %bitcast.43, bf16[32,80,128]{2,1,0:T(8,128)(2,1)} %reshape.174.in_ref, bf16[32,80,128]{2,1,0:T(8,128)(2,1)} %reshape.175.up_ref), custom_call_target="tpu_custom_call" | custom-call | tf_op jit(solution)/shard_map/dispatch/pallas_call | solution.py:196
  115.7 1.4 reshape.176
  117.0 1.9 fusion.3
  119.0 0.0 copy-start.2
  119.0 2.0 fusion.8
  120.9 0.0 copy-done.2
  121.0 0.3 reshape.179
  121.2 2.1 convolution_convert_fusion.1
  123.3 0.7 convolution_convert_fusion
  124.1 0.3 reshape.178.out_ref
  124.4 0.0 copy-start.3
  124.4 0.0 copy-start.4
  124.4 0.0 copy-start.5
  124.4 66.5 %give_back.1 = (bf16[32,80,128]{2,1,0:T(8,128)(2,1)S(1)}, f32[64,384]{1,0:T(8,128)S(1)}) custom-call(bf16[32,80,128]{2,1,0:T(8,128)(2,1)S(1)} %reshape.178.out_ref, bf16[4,4,2,64,384]{4,3,2,1,0:T(8,128)(2,1)S(1)} %bitcast.41), custom_call_target="tpu_custom_call" | custom-call | tf_op jit(solution)/shard_map/give_back/pallas_call | solution.py:307
  191.0 0.0 copy-done.3
  191.0 0.0 copy-done.4
  191.0 0.0 copy-done.5
  191.0 0.1 subtract_convert_fusion
  191.2 0.8 pad_maximum_fusion
  192.0 31.7 %all-to-all-start = ((bf16[32,2,1152]{2,1,0:T(2,128)(2,1)}), bf16[32,2,1152]{2,1,0:T(2,128)(2,1)S(1)}, u32[]{:S(2)}, u32[]{:S(2)}) async-start(bf16[32,2,1152]{2,1,0:T(2,128)(2,1)} %pad_maximum_fusion), calls=%async_computation | async-start | bytes 294912 | tf_op jit(solution)/shard_map/all_to_all | solution.py:412
  223.7 13.3 %all-to-all-done = bf16[32,2,1152]{2,1,0:T(2,128)(2,1)S(1)} async-done(((bf16[32,2,1152]{2,1,0:T(2,128)(2,1)}), bf16[32,2,1152]{2,1,0:T(2,128)(2,1)S(1)}, u32[]{:S(2)}, u32[]{:S(2)}) %all-to-all-start) | async-done | bytes 147488 | tf_op jit(solution)/shard_map/all_to_all | solution.py:412
  237.0 0.9 gather_fusion.1
  237.9 0.9 broadcast_select_fusion.1
  238.8 4.8 %all-to-all-start.1 = ((bf16[32,2,1152]{2,1,0:T(2,128)(2,1)}), bf16[32,2,1152]{2,1,0:T(2,128)(2,1)S(1)}, u32[]{:S(2)}, u32[]{:S(2)}) async-start(bf16[32,2,1152]{2,1,0:T(2,128)(2,1)} %broadcast_select_fusion.1), calls=%async_computation.1 | async-start | bytes 294912 | tf_op jit(solution)/shard_map/all_to_all | solution.py:414
  243.6 0.3 reshape.181
  243.9 0.0 copy-start.1
  243.9 0.0 copy-start.6
  243.9 0.9 gather_fusion
  244.9 0.1 copy-done.1
  244.9 0.0 copy-done.6
  244.9 1.6 fusion.13
  246.5 10.4 %all-to-all-done.1 = bf16[32,2,1152]{2,1,0:T(2,128)(2,1)S(1)} async-done(((bf16[32,2,1152]{2,1,0:T(2,128)(2,1)}), bf16[32,2,1152]{2,1,0:T(2,128)(2,1)S(1)}, u32[]{:S(2)}, u32[]{:S(2)}) %all-to-all-start.1) | async-done | bytes 147488 | tf_op jit(solution)/shard_map/all_to_all | solution.py:414
  256.9 0.1 reshape.182
  257.1 0.2 slice_bitcast_fusion
  257.3 0.6 copy.19
  258.0 0.6 copy.20
  258.6 0.6 copy.21
  259.2 0.6 copy.23
  (9 shorter events, 0.1 us)
Async XLA Ops:
  0.6 5.3 %copy-start = (bf16[128,2048]{1,0:T(8,128)(2,1)S(1)}, bf16[128,2048]{1,0:T(8,128)(2,1)}, u32[]{:S(2)}) copy-start(bf16[128,2048]{1,0:T(8,128)(2,1)} %param.10) | copy-start | bytes 1572868
  119.0 2.0 copy-start.2
  124.4 66.6 %copy-start.3 = (f32[1,64,384]{2,1,0:T(8,128)S(1)}, f32[1,64,384]{2,1,0:T(8,128)}, u32[]{:S(2)}) copy-start(f32[1,64,384]{2,1,0:T(8,128)} %param.15) | copy-start | bytes 294916
  124.4 66.6 %copy-start.4 = (f32[1,64,384]{2,1,0:T(8,128)S(1)}, f32[1,64,384]{2,1,0:T(8,128)}, u32[]{:S(2)}) copy-start(f32[1,64,384]{2,1,0:T(8,128)} %param.16) | copy-start | bytes 294916
  124.4 66.6 %copy-start.5 = (f32[1,64,384]{2,1,0:T(8,128)S(1)}, f32[1,64,384]{2,1,0:T(8,128)}, u32[]{:S(2)}) copy-start(f32[1,64,384]{2,1,0:T(8,128)} %param.17) | copy-start | bytes 294916
  192.0 45.1 %all-to-all-start = ((bf16[32,2,1152]{2,1,0:T(2,128)(2,1)}), bf16[32,2,1152]{2,1,0:T(2,128)(2,1)S(1)}, u32[]{:S(2)}, u32[]{:S(2)}) async-start(bf16[32,2,1152]{2,1,0:T(2,128)(2,1)} %pad_maximum_fusion), calls=%async_computation | async-start | bytes 294912 | tf_op jit(solution)/shard_map/all_to_all | solution.py:412
  238.8 18.2 %all-to-all-start.1 = ((bf16[32,2,1152]{2,1,0:T(2,128)(2,1)}), bf16[32,2,1152]{2,1,0:T(2,128)(2,1)S(1)}, u32[]{:S(2)}, u32[]{:S(2)}) async-start(bf16[32,2,1152]{2,1,0:T(2,128)(2,1)} %broadcast_select_fusion.1), calls=%async_computation.1 | async-start | bytes 294912 | tf_op jit(solution)/shard_map/all_to_all | solution.py:414
  243.9 1.0 copy-start.1
  243.9 1.0 copy-start.6

commit v2 on v1

--- a/solution.py
+++ b/solution.py
@@ -212,17 +212,39 @@
     )(weight, send_in, send_up)
 
 
+def middle(q, core):
+    z = 2 + 2 * (q // RING)
+    return (z + core * (7 - 2 * z)) * RING + q % RING
+
+
+def middle_of(ex, core):
+    z = ex // RING
+    z = z + core * (7 - 2 * z)
+    return (z % 2 == 0) & (z >= 2), (z // 2 - 1) * RING + ex % RING
+
+
 def give_back_kernel(
     experts,
     out_ref,
     partial_ref,
+    master_ref,
+    first_ref,
+    second_ref,
+    source_ref,
     returned_ref,
     grads_ref,
+    new_master_ref,
+    new_first_ref,
+    new_second_ref,
     c_buf,
     y_from,
     y_buf,
     z_from,
     z_buf,
+    state,
+    spread,
+    ordered,
+    arrived,
     local_sem,
     out_send,
     out_recv,
@@ -232,6 +254,10 @@
     y_recv,
     z_send,
     z_recv,
+    s_send,
+    s_recv,
+    t_send,
+    t_recv,
 ):
     dp, ex, z, y, core = place()
     sibling = (index_of(z, y, 1 - core), ex)
@@ -291,45 +317,130 @@
         copy.start()
     for copy in z_copies:
         copy.wait()
-    total = z_from[z].astype(jnp.float32)
+    grads = z_from[z].astype(jnp.float32)
     for s in range(RING - 1):
-        total += z_buf[s].astype(jnp.float32)
-    grads_ref[...] = total
+        grads += z_buf[s].astype(jnp.float32)
+    grads_ref[...] = grads
+    first = beta_first * first_ref[...] + (1.0 - beta_first) * grads
+    second = beta_second * second_ref[...] + (1.0 - beta_second) * grads * grads
+    updated = master_ref[...] - learn_rate * first / (jnp.sqrt(second) + adam_eps)
+    tall, wide = state.shape[2:]
+    pieces = state.shape[0]
+    across = grads.shape[1] // wide
+
+    def piece(q):
+        return pl.ds(q // across * tall, tall), pl.ds(q % across * wide, wide)
+
+    for i, value in enumerate((updated, first, second)):
+        value = value.astype(state.dtype)
+        for q in range(pieces):
+            row, column = q // across * tall, q % across * wide
+            state[q, i] = value[row : row + tall, column : column + wide]
+
+    is_middle, mine = middle_of(ex, core)
+
+    def spread_copy(q):
+        return send(
+            state.at[q], spread.at[ex], s_send.at[q], s_recv.at[ex], (dp, middle(q, core))
+        )
+
+    for q in range(pieces):
+
+        @pl.when(middle(q, core) != ex)
+        def _(q=q):
+            spread_copy(q).start()
+
+    def order_copy(step):
+        target = (ex + step) % experts
+        return send(
+            ordered.at[target], arrived.at[mine], t_send.at[target], t_recv.at[mine], (dp, target)
+        )
+
+    @pl.when(is_middle)
+    def _():
+        spread[ex] = state[mine]
+
+        def landed(step, carry):
+            other = (ex + step) % experts
+            there = spread.at[other]
+            send(there, there, s_send.at[0], s_recv.at[other], (dp, other)).wait_recv()
+            return carry
+
+        def pick(e, carry):
+            ordered[e] = spread[source_ref[e]]
+            return carry
+
+        def start(step, carry):
+            order_copy(step).start()
+            return carry
+
+        lax.fori_loop(1, experts, landed, 0)
+        lax.fori_loop(0, experts, pick, 0)
+        lax.fori_loop(1, experts, start, 0)
+        arrived[mine] = ordered[ex]
+
+    for q in range(pieces):
+        there = arrived.at[q]
+
+        @pl.when(middle(q, core) != ex)
+        def _(q=q, there=there):
+            spread_copy(q).wait_send()
+            send(
+                there, there, t_send.at[0], t_recv.at[q], (dp, middle(q, core))
+            ).wait_recv()
+
+    for q in range(pieces):
+        for i, ref in enumerate((new_master_ref, new_first_ref, new_second_ref)):
+            ref[piece(q)] = arrived[q, i].astype(ref.dtype)
+
+    @pl.when(is_middle)
+    def _():
+        def sent(step, carry):
+            order_copy(step).wait_send()
+            return carry
+
+        lax.fori_loop(1, experts, sent, 0)
+
     finish_out()
     own.wait()
 
 
-def give_back(outputs, partial):
+def give_back(outputs, partial, master, first_moment, second_moment, source):
     experts = outputs.shape[0]
     dma = pltpu.SemaphoreType.DMA
-    rows, width = partial.shape[3:]
-    block = (rows, width)
+    block = partial.shape[3:]
+    kind = partial.dtype
+    piece = (3, 16, 128)
+    pieces = block[0] * block[1] // (16 * 128)
     return pl.pallas_call(
         functools.partial(give_back_kernel, experts),
-        out_shape=[
-            jax.ShapeDtypeStruct(outputs.shape, outputs.dtype),
-            jax.ShapeDtypeStruct(block, jnp.float32),
-        ],
-        in_specs=[ANY, VMEM],
-        out_specs=[ANY, VMEM],
+        out_shape=[jax.ShapeDtypeStruct(outputs.shape, outputs.dtype)]
+        + [jax.ShapeDtypeStruct(block, jnp.float32)] * 4,
+        in_specs=[ANY] + [VMEM] * 4 + [pl.BlockSpec(memory_space=pltpu.SMEM)],
+        out_specs=[ANY] + [VMEM] * 4,
         scratch_shapes=[
-            pltpu.VMEM((RING, RING) + block, partial.dtype),
-            pltpu.VMEM((RING, RING) + block, partial.dtype),
-            pltpu.VMEM((RING - 1, RING) + block, partial.dtype),
-            pltpu.VMEM((RING,) + block, partial.dtype),
-            pltpu.VMEM((RING - 1,) + block, partial.dtype),
+            pltpu.VMEM((RING, RING) + block, kind),
+            pltpu.VMEM((RING, RING) + block, kind),
+            pltpu.VMEM((RING - 1, RING) + block, kind),
+            pltpu.VMEM((RING,) + block, kind),
+            pltpu.VMEM((RING - 1,) + block, kind),
+            pltpu.VMEM((pieces,) + piece, kind),
+            pltpu.VMEM((experts,) + piece, kind),
+            pltpu.VMEM((experts,) + piece, kind),
+            pltpu.VMEM((pieces,) + piece, kind),
             dma,
             dma((experts,)),
             dma((experts,)),
             dma,
             dma,
         ]
-        + [dma((RING - 1,))] * 4,
+        + [dma((RING - 1,))] * 4
+        + [dma((pieces,)), dma((experts,)), dma((experts,)), dma((pieces,))],
         compiler_params=pltpu.CompilerParams(
             collective_id=1, has_side_effects=True, vmem_limit_bytes=24 * 1024 * 1024
         ),
         name="give_back",
-    )(outputs, partial)
+    )(outputs, partial, master, first_moment, second_moment, source)
 
 
 def shards(
@@ -390,8 +501,16 @@
         preferred_element_type=jnp.float32,
     ).astype(jnp.bfloat16)
     partial = contract_rows(recv_up, hidden).astype(jnp.bfloat16)
-    returned, grads = give_back(
-        outputs.reshape(packed), partial.reshape(RING, RING, CORES, -1, ff_width)
+    source_slot = jnp.sum(
+        expert_range[None, :] * (old_place[None, :] == new_place[:, None]).astype(jnp.int32), axis=1
+    )
+    returned, *state = give_back(
+        outputs.reshape(packed),
+        partial.reshape(RING, RING, CORES, -1, ff_width),
+        master[0],
+        first_moment[0],
+        second_moment[0],
+        source_slot,
     )
     returned = returned.reshape(slots, model)
     picked = (
@@ -399,21 +518,7 @@
     )
     combined = jnp.sum(route_gates[:, :, None] * picked, axis=1).astype(jnp.bfloat16)
     gate_grads = jnp.sum(cotangent[:, None, :].astype(jnp.float32) * picked, axis=2)
-    grads = grads[None]
-    first = beta_first * first_moment + (1.0 - beta_first) * grads
-    second = beta_second * second_moment + (1.0 - beta_second) * grads * grads
-    updated = master - learn_rate * first / (jnp.sqrt(second) + adam_eps)
-    source_slot = jnp.sum(
-        expert_range[None, :] * (old_place[None, :] == new_place[:, None]).astype(jnp.int32), axis=1
-    )
-    state = jnp.concatenate([updated, first, second], axis=2).astype(jnp.bfloat16)
-    rows = state.shape[1]
-    state = state.reshape(experts, rows // experts, -1)
-    spread = lax.all_to_all(state, "expert", split_axis=0, concat_axis=0, tiled=True)
-    ordered = jnp.take(spread, source_slot, axis=0)
-    moved = lax.all_to_all(ordered, "expert", split_axis=0, concat_axis=0, tiled=True)
-    moved = moved.reshape(1, rows, 3, ff_width).astype(jnp.float32)
-    return (combined, gate_grads, grads, moved[:, :, 0], moved[:, :, 1], moved[:, :, 2])
+    return (combined, gate_grads) + tuple(value[None] for value in state)
 
 
 def solution(mesh):

time: 262 us -> 247 us (0.943)
  Pallas kernels: 175 us -> 215 us
  starting transfers between devices: 36.5 us -> 0 us
  waiting for transfers between devices: 23.7 us -> 0 us
  local copies, waits for them, and re-layouts: 9.49 us -> 12.5 us
    pallas_call x1, Pallas kernels: 66.5 us -> 107 us  [give_back(): pl.pallas_call(functools.partial(give_back_kernel, experts), out_shape=[j...]
    all_to_all x2 -> x0, starting transfers between devices: 36.5 us -> none  [the longest x1 31.7 us: shards(): lax.all_to_all(state, 'expert', split_axis=0, concat_axis=0, tiled=True)]
    all_to_all x2 -> x0, waiting for transfers between devices: 23.7 us -> none  [the longest x1 13.3 us: shards(): lax.all_to_all(state, 'expert', split_axis=0, concat_axis=0, tiled=True)]
    unnamed x18 -> x36, local copies, waits for them, and re-layouts: 2.71 us -> 6.98 us
  transfers between devices with their start and end apart: 2 -> 0, of which waited for: 2 -> 0; matrix products, arithmetic and copies ran while one was open for 1% -> 0% of each run, Pallas kernels for 0% -> 0%
where the time goes in v2:
time: 247 us; the launch traced here: 243 us
  Pallas kernels  215 us (87%)
  local copies, waits for them, and re-layouts  12.5 us (5%)
  matrix products  10.1 us (4%)
  other arithmetic  4.27 us (2%)
    pallas_call x1, Pallas kernels, dispatch(): pl.pallas_call(functools.partial(dispatch_kernel, experts), out_shape=[ja...  108 us
    pallas_call x1, Pallas kernels, give_back(): pl.pallas_call(functools.partial(give_back_kernel, experts), out_shape=[j...  107 us
    unnamed x36, local copies, waits for them, and re-layouts  6.98 us

profile of v2, /device:TPU:24, one launch (start us, length us, event | category | flops | bytes accessed | tf_op | source)
XLA Modules:
  0.0 243.0 jit_solution(319116473177854347)
XLA Ops:
  0.6 0.0 copy-start
  0.6 0.8 fusion.16
  1.4 0.2 reduce_window_sum.11
  1.6 0.8 select_reduce_fusion.2
  2.5 0.8 select_reduce_fusion.1
  3.3 1.4 convolution_convert_fusion.2
  4.8 1.2 reshape.119.up_ref
  6.0 0.0 copy-done
  6.0 0.3 convolution_convert_fusion.3
  6.3 1.1 reshape.118.in_ref
  7.5 108.2 %dispatch.1 = (bf16[32,64,1152]{2,1,0:T(8,128)(2,1)}, bf16[32,80,128]{2,1,0:T(8,128)(2,1)}, bf16[32,80,128]{2,1,0:T(8,128)(2,1)}) custom-call(bf16[64,1152]{1,0:T(8,128)(2,1)} %bitcast.31, bf16[32,80,128]{2,1,0:T(8,128)(2,1)} %reshape.118.in_ref, bf16[32,80,128]{2,1,0:T(8,128)(2,1)} %reshape.119.up_ref), custom_call_target="tpu_custom_call" | custom-call | tf_op jit(solution)/shard_map/dispatch/pallas_call | solution.py:196
  115.7 1.4 reshape.120
  117.0 1.9 fusion.3
  119.0 0.0 copy-start.13
  119.0 2.6 %fusion.8 = bf16[160,384]{1,0:T(8,128)(2,1)} fusion(bf16[160,2048]{1,0:T(8,128)(2,1)S(1)} %reshape.120, bf16[2048,1152]{1,0:T(8,128)(2,1)} %bitcast.38, f32[160,384]{1,0:T(8,128)S(1)} %fusion.3), kind=kOutput, calls=%fused_computation.14 | convolution fusion | flops 252026880 | bytes 2596864 | tf_op jit(solution)/shard_map/dot_general | solution.py:493
  121.6 0.0 copy-done.13
  121.6 0.3 reshape.123
  121.9 0.0 copy-start.14
  121.9 1.7 convolution_convert_fusion
  123.6 0.0 copy-done.14
  123.6 0.0 copy-start.1
  123.6 2.1 convolution_convert_fusion.1
  125.8 0.3 reshape.122.out_ref
  126.1 0.0 copy-done.1
  126.1 0.0 copy-start.2
  126.1 0.9 copy-done.2
  127.0 0.0 copy-start.3
  127.0 0.9 copy-done.3
  127.9 107.1 %give_back.1 = (bf16[32,80,128]{2,1,0:T(8,128)(2,1)S(1)}, f32[64,384]{1,0:T(8,128)S(1)}, f32[64,384]{1,0:T(8,128)S(1)}, f32[64,384]{1,0:T(8,128)S(1)}, f32[64,384]{1,0:T(8,128)S(1)}) custom-call(bf16[32,80,128]{2,1,0:T(8,128)(2,1)S(1)} %reshape.122.out_ref, bf16[4,4,2,64,384]{4,3,2,1,0:T(8,128)(2,1)S(1)} %bitcast.23, f32[64,384]{1,0:T(8,128)S(1)} %bitcast.24, ...), custom_call_target="tpu_custom_call" | custom-call | tf_op jit(solution)/shard_map/give_back/pallas_call | solution.py:415
  234.9 0.0 copy-start.4
  234.9 0.6 copy-done.4
  235.6 0.0 copy-start.6
  235.6 0.6 copy-done.6
  236.2 0.0 copy-start.8
  236.2 0.6 copy-done.8
  236.9 0.0 copy-start.10
  236.9 0.6 copy-done.10
  237.5 0.3 reshape.125
  237.8 0.0 copy-start.12
  237.8 0.0 copy-start.15
  237.8 0.9 gather_fusion
  238.8 0.0 copy-start.11
  238.8 0.0 copy-start.9
  238.8 0.0 copy-start.7
  238.8 0.0 copy-start.5
  238.8 0.0 copy-done.12
  238.8 0.0 copy-done.15
  238.8 1.6 fusion.13
  240.4 0.0 copy-done.11
  240.4 0.6 copy.20
  241.1 0.0 copy-done.9
  241.1 0.6 copy.21
  241.7 0.0 copy-done.7
  241.7 0.6 copy.22
  242.4 0.0 copy-done.5
  242.4 0.6 copy.23
  (3 shorter events, 0.0 us)
Async XLA Ops:
  0.6 5.3 %copy-start = (bf16[128,2048]{1,0:T(8,128)(2,1)S(1)}, bf16[128,2048]{1,0:T(8,128)(2,1)}, u32[]{:S(2)}) copy-start(bf16[128,2048]{1,0:T(8,128)(2,1)} %param.10) | copy-start | bytes 1572868
  119.0 2.6 %copy-start.13 = (bf16[32,80,128]{2,1,0:T(8,128)(2,1)S(1)}, bf16[32,80,128]{2,1,0:T(8,128)(2,1)}, u32[]{:S(2)}) copy-start(bf16[32,80,128]{2,1,0:T(8,128)(2,1)} %get-tuple-element.16) | copy-start | bytes 1966084
  121.9 1.7 copy-start.14
  123.6 2.4 %copy-start.1 = (f32[1,64,384]{2,1,0:T(8,128)S(1)}, f32[1,64,384]{2,1,0:T(8,128)}, u32[]{:S(2)}) copy-start(f32[1,64,384]{2,1,0:T(8,128)} %param.15) | copy-start | bytes 294916
  126.1 0.9 copy-start.2
  127.0 0.9 copy-start.3
  234.9 0.6 copy-start.4
  235.6 0.6 copy-start.6
  236.2 0.6 copy-start.8
  236.9 0.6 copy-start.10
  237.8 1.0 copy-start.12
  237.8 1.0 copy-start.15
  238.8 1.7 copy-start.11
  238.8 2.3 copy-start.9
  238.8 2.9 %copy-start.7 = (f32[64,384]{1,0:T(8,128)S(1)}, f32[64,384]{1,0:T(8,128)}, u32[]{:S(2)}) copy-start(f32[64,384]{1,0:T(8,128)} %copy-done.6) | copy-start | bytes 294916
  238.8 3.6 %copy-start.5 = (f32[64,384]{1,0:T(8,128)S(1)}, f32[64,384]{1,0:T(8,128)}, u32[]{:S(2)}) copy-start(f32[64,384]{1,0:T(8,128)} %copy-done.4) | copy-start | bytes 294916

commit v3 on v2

v3 whole, which is shorter than its diff:
```python
import functools

import jax
import jax.numpy as jnp
from jax import lax
from jax.experimental import pallas as pl
from jax.experimental.pallas import tpu as pltpu
from jax.sharding import PartitionSpec as P

beta_first = 0.9
beta_second = 0.999
learn_rate = 0.01
adam_eps = 1e-08

MESH = pl.DeviceIdType.MESH
VMEM = pl.BlockSpec(memory_space=pltpu.VMEM)
RING = 4
CORES = 2


def silu_value(values):
    return values * jax.nn.sigmoid(values)


def contract_rows(left, right):
    return lax.dot_general(
        left, right, (((0,), (0,)), ((), ())), preferred_element_type=jnp.float32
    )


def place():
    dp, ex = lax.axis_index("dp"), lax.axis_index("expert")
    return dp, ex, dp // (RING * CORES), (dp // CORES) % RING, dp % CORES


def index_of(z, y, core):
    return ((z % RING) * RING + y % RING) * CORES + core


def send(src, dst, send_sem, recv_sem, device):
    return pltpu.make_async_remote_copy(
        src_ref=src,
        dst_ref=dst,
        send_sem=send_sem,
        recv_sem=recv_sem,
        device_id=device,
        device_id_type=MESH,
    )


def greet(devices, experts, dp, ex):
    barrier = pltpu.get_barrier_semaphore()
    for device in devices:
        pl.semaphore_signal(barrier, inc=1, device_id=device, device_id_type=MESH)

    def one(step, carry):
        pl.semaphore_signal(
            barrier, inc=1, device_id=(dp, (ex + step) % experts), device_id_type=MESH
        )
        return carry

    lax.fori_loop(1, experts, one, 0)
    return lambda: pl.semaphore_wait(barrier, len(devices) + experts - 1)


def exchange(experts, dp, ex, src, dst, send_sems, recv_sems):
    def copy(step):
        target = (ex + step) % experts
        return send(
            src.at[target], dst.at[ex], send_sems.at[target], recv_sems.at[ex], (dp, target)
        )

    def start(step, carry):
        copy(step).start()
        return carry

    def arrival(step, carry):
        other = (ex + step) % experts
        there = dst.at[other]
        send(there, there, send_sems.at[other], recv_sems.at[other], (dp, other)).wait_recv()
        return carry

    def departure(step, carry):
        copy(step).wait_send()
        return carry

    lax.fori_loop(1, experts, start, 0)
    return (
        lambda: lax.fori_loop(1, experts, arrival, 0),
        lambda: lax.fori_loop(1, experts, departure, 0),
    )


def middle(q, core):
    z = 2 + 2 * (q // RING)
    return (z + core * (7 - 2 * z)) * RING + q % RING


def middle_of(ex, core):
    z = ex // RING
    z = z + core * (7 - 2 * z)
    return (z % 2 == 0) & (z >= 2), (z // 2 - 1) * RING + ex % RING


def layer_kernel(
    experts,
    place_ref,
    pick_ref,
    gates_ref,
    tokens_ref,
    cot_ref,
    weight_ref,
    master_ref,
    first_ref,
    second_ref,
    source_ref,
    combined_ref,
    gate_grads_ref,
    grads_ref,
    new_master_ref,
    new_first_ref,
    new_second_ref,
    whole,
    pack,
    rows,
    both,
    hidden,
    in_from,
    in_to,
    up_from,
    up_to,
    out_from,
    out_to,
    partial,
    c_buf,
    y_from,
    y_buf,
    z_from,
    z_buf,
    state,
    spread,
    ordered,
    arrived,
    local_sem,
    in_send,
    in_recv,
    up_send,
    up_recv,
    out_send,
    out_recv,
    wz_send,
    wz_recv,
    wy_send,
    wy_recv,
    wc_send,
    wc_recv,
    c_send,
    c_recv,
    y_send,
    y_recv,
    z_send,
    z_recv,
    s_send,
    s_recv,
    t_send,
    t_recv,
):
    dp, ex, z, y, core = place()
    sibling = (index_of(z, y, 1 - core), ex)
    ring_y = [(index_of(z, y + s, core), ex) for s in range(1, RING)]
    ring_z = [(index_of(z + s, y, core), ex) for s in range(1, RING)]
    right, left = ring_z[0], ring_z[2]
    all_here = greet([sibling] + ring_y + ring_z, experts, dp, ex)

    slots, model = rows.shape
    depth = weight_ref.shape[0]
    half = depth // 2
    ff = hidden.shape[1]
    lanes = pack.shape[1]
    per_row = model // lanes
    block = in_from.shape[1]
    wide_step = 2 * lanes
    steps = model // wide_step

    def columns(i, width):
        return pl.ds(pl.multiple_of(i * width, width), width)

    def pack_column(c, value):
        pack[pl.ds(c, slots, stride=per_row), :] = value

    def to_blocks(dst):
        def one(i, carry):
            dst[i] = pack[columns(i, block), :].astype(dst.dtype)
            return carry

        lax.fori_loop(0, experts, one, 0)

    def to_rows(src):
        def one(i, carry):
            pack[columns(i, block), :] = src[i].astype(jnp.float32)
            return carry

        def other(c, carry):
            rows[:, columns(c, lanes)] = pack[pl.ds(c, slots, stride=per_row), :].astype(rows.dtype)
            return carry

        lax.fori_loop(0, experts, one, 0)
        lax.fori_loop(0, per_row, other, 0)

    def place_in(c, carry):
        value = tokens_ref[:, columns(c, lanes)]
        pack_column(c, jnp.dot(place_ref[...], value, preferred_element_type=jnp.float32))
        return carry

    def place_up(c, carry):
        value = gates_ref[...] * cot_ref[:, columns(c, lanes)].astype(jnp.float32)
        value = value.astype(cot_ref.dtype)
        pack_column(c, jnp.dot(place_ref[...], value, preferred_element_type=jnp.float32))
        return carry

    lax.fori_loop(0, per_row, place_in, 0)
    to_blocks(in_from)
    all_here()

    sent = []

    def start(copy):
        copy.start()
        sent.append(copy)

    def slot(index, first=0, count=depth):
        return whole.at[pl.ds(pl.multiple_of(index * depth + first, half), count), :]

    blocks = [dp, left[0], right[0], ring_z[1][0]]

    def z_copy(i, src, index, part, device):
        return send(src, slot(index, *part), wz_send.at[i], wz_recv.at[i], device)

    def z_arrival(i, index, part):
        there = slot(index, *part)
        send(there, there, wz_send.at[i], wz_recv.at[i], right).wait_recv()

    every, low, high = (0, depth), (0, half), (half, half)

    def spread_weight(k, src):
        for s in range(1, RING):
            start(
                send(
                    src,
                    slot(blocks[k]),
                    wy_send.at[k, s - 1],
                    wy_recv.at[k, s - 1],
                    ring_y[s - 1],
                )
            )
        start(send(src, slot(blocks[k]), wc_send.at[k, 0], wc_recv.at[k, 0], sibling))

    def pass_on(k):
        for s in range(1, RING):
            there = slot(index_of(blocks[k] // (RING * CORES), y + RING - s, core))
            send(there, there, wy_send.at[k, s - 1], wy_recv.at[k, s - 1], sibling).wait_recv()
            start(send(there, there, wc_send.at[k, s], wc_recv.at[k, s], sibling))

    own = pltpu.make_async_copy(weight_ref, slot(dp), local_sem)
    own.start()
    start(z_copy(0, weight_ref, dp, every, right))
    start(z_copy(1, weight_ref, dp, every, left))
    in_there, in_left = exchange(experts, dp, ex, in_from, in_to, in_send, in_recv)
    spread_weight(0, weight_ref)
    in_to[ex] = in_from[ex]
    lax.fori_loop(0, per_row, place_up, 0)
    to_blocks(up_from)
    up_there, up_left = exchange(experts, dp, ex, up_from, up_to, up_send, up_recv)
    up_to[ex] = up_from[ex]
    z_arrival(0, blocks[1], every)
    start(z_copy(2, slot(blocks[1], *low), blocks[1], low, right))
    spread_weight(1, slot(blocks[1]))
    z_arrival(1, blocks[2], every)
    start(z_copy(3, slot(blocks[2], *high), blocks[2], high, left))
    spread_weight(2, slot(blocks[2]))
    pass_on(0)
    z_arrival(2, blocks[3], low)
    z_arrival(3, blocks[3], high)
    spread_weight(3, slot(blocks[3]))
    in_there()
    to_rows(in_to)
    pass_on(1)
    pass_on(2)
    pass_on(3)
    for k in range(RING):
        for s in range(RING):
            there = slot(index_of(blocks[k] // (RING * CORES), y + RING - s, 1 - core))
            send(there, there, wc_send.at[k, s], wc_recv.at[k, s], sibling).wait_recv()
    own.wait()

    both[...] = jnp.zeros_like(both)

    def gate_up(i, carry):
        both[...] += jnp.dot(
            rows[:, columns(i, wide_step)],
            whole[columns(i, wide_step), pl.ds(0, 2 * ff)],
            preferred_element_type=jnp.float32,
        )
        return carry

    lax.fori_loop(0, steps, gate_up, 0)
    hidden[...] = (silu_value(both[:, :ff]) * both[:, ff:]).astype(hidden.dtype)

    def down(i, carry):
        value = lax.dot_general(
            hidden[...],
            whole[columns(i, wide_step), pl.ds(2 * ff, ff)],
            (((1,), (1,)), ((), ())),
            preferred_element_type=jnp.float32,
        )
        pack_column(2 * i, value[:, :lanes])
        pack_column(2 * i + 1, value[:, lanes:])
        return carry

    lax.fori_loop(0, steps, down, 0)
    to_blocks(out_from)
    out_there, out_left = exchange(experts, dp, ex, out_from, out_to, out_send, out_recv)
    out_to[ex] = out_from[ex]

    up_there()
    to_rows(up_to)
    pairs = wide_step // (CORES * depth)

    def grad(i, carry):
        value = contract_rows(rows[:, columns(i, wide_step)], hidden[...]).astype(partial.dtype)
        partial[pl.ds(i * pairs, pairs)] = value.reshape((pairs, CORES, depth, ff))
        return carry

    lax.fori_loop(0, steps, grad, 0)
    to_core = send(partial.at[:, 1 - core], c_buf, c_send, c_recv, sibling)
    to_core.start()
    to_core.wait()

    def pair(i, carry):
        at, row = i // RING, i % RING
        y_from[row, at] = (
            partial[i, core].astype(jnp.float32) + c_buf[i].astype(jnp.float32)
        ).astype(y_from.dtype)
        return carry

    lax.fori_loop(0, RING * RING, pair, 0)
    y_copies = [
        send(
            y_from.at[(y + s) % RING],
            y_buf.at[s - 1],
            y_send.at[s - 1],
            y_recv.at[s - 1],
            ring_y[s - 1],
        )
        for s in range(1, RING)
    ]
    for copy in y_copies:
        copy.start()
    for copy in y_copies:
        copy.wait()

    def quad(i, carry):
        total = y_from[y, i].astype(jnp.float32)
        for s in range(RING - 1):
            total += y_buf[s, i].astype(jnp.float32)
        z_from[i] = total.astype(z_from.dtype)
        return carry

    lax.fori_loop(0, RING, quad, 0)
    z_copies = [
        send(
            z_from.at[(z + s) % RING],
            z_buf.at[s - 1],
            z_send.at[s - 1],
            z_recv.at[s - 1],
            ring_z[s - 1],
        )
        for s in range(1, RING)
    ]
    for copy in z_copies:
        copy.start()
    for copy in z_copies:
        copy.wait()
    grads = z_from[z].astype(jnp.float32)
    for s in range(RING - 1):
        grads += z_buf[s].astype(jnp.float32)
    grads_ref[...] = grads
    first = beta_first * first_ref[...] + (1.0 - beta_first) * grads
    second = beta_second * second_ref[...] + (1.0 - beta_second) * grads * grads
    updated = master_ref[...] - learn_rate * first / (jnp.sqrt(second) + adam_eps)
    tall, wide = state.shape[2:]
    pieces = state.shape[0]
    across = grads.shape[1] // wide

    def piece(q):
        return pl.ds(q // across * tall, tall), pl.ds(q % across * wide, wide)

    for i, value in enumerate((updated, first, second)):
        value = value.astype(state.dtype)
        for q in range(pieces):
            row, column = q // across * tall, q % across * wide
            state[q, i] = value[row : row + tall, column : column + wide]

    is_middle, mine = middle_of(ex, core)

    def spread_copy(q):
        return send(
            state.at[q], spread.at[ex], s_send.at[q], s_recv.at[ex], (dp, middle(q, core))
        )

    for q in range(pieces):

        @pl.when(middle(q, core) != ex)
        def _(q=q):
            spread_copy(q).start()

    def order_copy(step):
        target = (ex + step) % experts
        return send(
            ordered.at[target], arrived.at[mine], t_send.at[target], t_recv.at[mine], (dp, target)
        )

    @pl.when(is_middle)
    def _():
        spread[ex] = state[mine]

        def landed(step, carry):
            other = (ex + step) % experts
            there = spread.at[other]
            send(there, there, s_send.at[0], s_recv.at[other], (dp, other)).wait_recv()
            return carry

        def pick(e, carry):
            ordered[e] = spread[source_ref[e]]
            return carry

        def start(step, carry):
            order_copy(step).start()
            return carry

        lax.fori_loop(1, experts, landed, 0)
        lax.fori_loop(0, experts, pick, 0)
        lax.fori_loop(1, experts, start, 0)
        arrived[mine] = ordered[ex]

    for q in range(pieces):
        there = arrived.at[q]

        @pl.when(middle(q, core) != ex)
        def _(q=q, there=there):
            spread_copy(q).wait_send()
            send(
                there, there, t_send.at[0], t_recv.at[q], (dp, middle(q, core))
            ).wait_recv()

    for q in range(pieces):
        for i, ref in enumerate((new_master_ref, new_first_ref, new_second_ref)):
            ref[piece(q)] = arrived[q, i].astype(ref.dtype)

    @pl.when(is_middle)
    def _():
        def sent(step, carry):
            order_copy(step).wait_send()
            return carry

        lax.fori_loop(1, experts, sent, 0)

    out_there()
    to_rows(out_to)

    def combine(c, total):
        value = jnp.dot(
            pick_ref[...], rows[:, columns(c, lanes)], preferred_element_type=jnp.float32
        )
        combined_ref[:, columns(c, lanes)] = (gates_ref[...] * value).astype(combined_ref.dtype)
        return total + cot_ref[:, columns(c, lanes)].astype(jnp.float32) * value

    total = lax.fori_loop(
        0, per_row, combine, jnp.zeros((tokens_ref.shape[0], lanes), jnp.float32)
    )
    gate_grads_ref[...] = jnp.sum(total, axis=1, keepdims=True)
    for copy in sent:
        copy.wait_send()
    in_left()
    up_left()
    out_left()


def layer(place_slots, gates, tokens, cotangent, weight, state, source):
    slots, tok_rows = place_slots.shape
    model = tokens.shape[1]
    experts = source.shape[0]
    depth, ff = weight.shape[0], weight.shape[1] // 3
    dma = pltpu.SemaphoreType.DMA
    kind = tokens.dtype
    lanes = 128
    packed = (experts, slots * model // lanes // experts, lanes)
    block = (depth, ff)
    piece = (3, 16, 128)
    pieces = depth * ff // (16 * 128)

    def sixteen(*shape):
        return pltpu.VMEM(shape, kind)

    return pl.pallas_call(
        functools.partial(layer_kernel, experts),
        out_shape=[
            jax.ShapeDtypeStruct(tokens.shape, kind),
            jax.ShapeDtypeStruct((tok_rows, 1), jnp.float32),
        ]
        + [jax.ShapeDtypeStruct(block, jnp.float32)] * 4,
        in_specs=[VMEM] * 9 + [pl.BlockSpec(memory_space=pltpu.SMEM)],
        out_specs=[VMEM] * 6,
        scratch_shapes=[
            sixteen(model, 3 * ff),
            pltpu.VMEM((slots * model // lanes, lanes), jnp.float32),
            sixteen(slots, model),
            pltpu.VMEM((slots, 2 * ff), jnp.float32),
            sixteen(slots, ff),
        ]
        + [sixteen(*packed)] * 6
        + [
            sixteen(RING * RING, CORES, *block),
            sixteen(RING * RING, *block),
            sixteen(RING, RING, *block),
            sixteen(RING - 1, RING, *block),
            sixteen(RING, *block),
            sixteen(RING - 1, *block),
            sixteen(pieces, *piece),
            sixteen(experts, *piece),
            sixteen(experts, *piece),
            sixteen(pieces, *piece),
            dma,
        ]
        + [dma((experts,))] * 6
        + [dma((RING,))] * 2
        + [dma((RING, RING - 1))] * 2
        + [dma((RING, RING))] * 2
        + [dma] * 2
        + [dma((RING - 1,))] * 4
        + [dma((pieces,)), dma((experts,)), dma((experts,)), dma((pieces,))],
        compiler_params=pltpu.CompilerParams(
            collective_id=0, has_side_effects=True, vmem_limit_bytes=40 * 1024 * 1024
        ),
        name="layer",
    )(place_slots, place_slots.T, gates, tokens, cotangent, weight, *state, source)


def shards(
    tokens,
    route_ids,
    route_gates,
    cotangent,
    expert_weights,
    master,
    first_moment,
    second_moment,
    old_place,
    new_place,
):
    experts = lax.axis_size("expert")
    tok_rows = tokens.shape[0]
    routes = route_ids.shape[1]
    capacity = 5 * tok_rows * routes // (4 * experts)
    slots = experts * capacity
    expert_range = jnp.arange(experts, dtype=jnp.int32)
    holder = jnp.sum(
        expert_range[None, :] * (old_place[None, :] == expert_range[:, None]).astype(jnp.int32),
        axis=1,
    )
    flat_ids = route_ids.reshape(-1)
    onehot = (flat_ids[:, None] == expert_range[None, :]).astype(jnp.int32)
    rank_in = jnp.sum((jnp.cumsum(onehot, axis=0) - onehot) * onehot, axis=1)
    target = jnp.sum(onehot * holder[None, :], axis=1)
    slot_index = target * capacity + rank_in
    slot_range = jnp.arange(slots, dtype=jnp.int32)
    place_pairs = (slot_range[:, None] == slot_index[None, :]).astype(jnp.bfloat16)
    source_slot = jnp.sum(
        expert_range[None, :] * (old_place[None, :] == new_place[:, None]).astype(jnp.int32), axis=1
    )
    combined, gate_grads, *state = layer(
        place_pairs,
        route_gates,
        tokens,
        cotangent,
        expert_weights[0],
        (master[0], first_moment[0], second_moment[0]),
        source_slot,
    )
    return (combined, gate_grads) + tuple(value[None] for value in state)


def solution(mesh):
    in_specs = (
        P(("dp", "expert"), None),
        P(("dp", "expert"), None),
        P(("dp", "expert"), None),
        P(("dp", "expert"), None),
        P("expert", "dp", None),
        P("expert", "dp", None),
        P("expert", "dp", None),
        P("expert", "dp", None),
        P(),
        P(),
    )
    out_specs = (
        P(("dp", "expert"), None),
        P(("dp", "expert"), None),
        P("expert", "dp", None),
        P("expert", "dp", None),
        P("expert", "dp", None),
        P("expert", "dp", None),
    )
    return jax.shard_map(shards, mesh=mesh, in_specs=in_specs, out_specs=out_specs, check_vma=False)
```

time: 247 us -> 222 us (0.90)
  matrix products: 10.1 us -> 0 us
  Pallas kernels: 215 us -> 210 us
  local copies, waits for them, and re-layouts: 12.5 us -> 8.14 us
  other arithmetic: 4.27 us -> 0.71 us
    dot_general x6 -> x0, matrix products: 10.1 us -> none  [the longest x1 2.63 us: shards(): jnp.dot(recv_in, weight[:, ff_width:2 * ff_width], preferred_element_type...]
    pallas_call x2 -> x1, Pallas kernels: 215 us -> 210 us  [layer(): pl.pallas_call(functools.partial(layer_kernel, experts), out_shape=[jax.S...]
    reshape x6 -> x0, local copies, waits for them, and re-layouts: 4.56 us -> none  [the longest x1 1.37 us: shards(): recv_in = recv_in.reshape(slots, model)]
    unnamed x36 -> x27, local copies, waits for them, and re-layouts: 6.98 us -> 8.14 us
where the time goes in v3:
time: 222 us; the launch traced here: 220 us
  Pallas kernels  210 us (95%)
  local copies, waits for them, and re-layouts  8.14 us (4%)
    pallas_call x1, Pallas kernels, layer(): pl.pallas_call(functools.partial(layer_kernel, experts), out_shape=[jax.S...  210 us
    unnamed x27, local copies, waits for them, and re-layouts  8.14 us

profile of v3, /device:TPU:24, one launch (start us, length us, event | category | flops | bytes accessed | tf_op | source)
XLA Modules:
  0.0 219.7 jit_solution(1188575384927023373)
XLA Ops:
  0.6 0.0 copy-start.8
  0.6 0.0 copy-start.9
  0.7 0.6 copy-done.8
  1.3 0.0 copy-done.9
  1.3 0.2 select_reduce_fusion.2
  1.5 0.0 copy-start.6
  1.5 0.7 copy-done.6
  2.1 0.0 copy-start.5
  2.1 0.1 fusion.2
  2.2 0.0 copy-start.4
  2.2 0.2 reduce_window_sum.11
  2.4 0.0 copy-start.7
  2.4 0.0 copy-start.2
  2.4 0.2 select_reduce_fusion.1
  2.6 0.0 copy-start.3
  2.7 0.1 fusion.pick_ref
  2.8 0.3 copy-done.7
  3.1 0.1 copy.18.gates_ref
  3.2 0.0 copy-done.5
  3.2 0.0 copy-done.4
  3.2 0.2 copy-done.2
  3.4 0.2 copy-done.3
  3.6 0.0 copy-start
  3.6 1.0 copy-done
  4.6 0.0 copy-start.1
  4.6 1.0 copy-done.1
  5.6 210.1 %layer.1 = (bf16[128,2048]{1,0:T(8,128)(2,1)S(1)}, f32[128,1]{1,0:T(8,128)S(1)}, f32[64,384]{1,0:T(8,128)S(1)}, f32[64,384]{1,0:T(8,128)S(1)}, f32[64,384]{1,0:T(8,128)S(1)}, /*index=5*/f32[64,384]{1,0:T(8,128)S(1)}) custom-call(bf16[160,128]{1,0:T(8,128)(2,1)S(1)} %fusion.1.place_ref, bf16[128,160]{1,0:T(8,128)(2,1)S(1)} %fusion.pick_ref, ...), custom_call_target="tpu_custom_call" | custom-call | tf_op jit(solution)/shard_map/layer/pallas_call | solution.py:505
  215.8 0.6 copy.19
  216.4 0.8 copy.25
  217.2 0.6 copy.26
  217.8 0.6 copy.27
  218.5 0.6 copy.28
  219.1 0.6 copy.29
  (2 shorter events, 0.0 us)
Async XLA Ops:
  0.6 0.7 copy-start.8
  0.6 0.7 copy-start.9
  1.5 0.7 copy-start.6
  2.1 1.0 copy-start.5
  2.2 1.0 copy-start.4
  2.4 0.7 copy-start.7
  2.4 0.9 copy-start.2
  2.6 0.9 copy-start.3
  3.6 1.0 copy-start
  4.6 1.0 copy-start.1

commit v4 on v3

--- a/solution.py
+++ b/solution.py
@@ -121,8 +121,10 @@
     new_first_ref,
     new_second_ref,
     whole,
+    whole_down,
     pack,
     rows,
+    rows_up,
     both,
     hidden,
     in_from,
@@ -154,6 +156,12 @@
     wy_recv,
     wc_send,
     wc_recv,
+    dz_send,
+    dz_recv,
+    dy_send,
+    dy_recv,
+    dc_send,
+    dc_recv,
     c_send,
     c_recv,
     y_send,
@@ -174,51 +182,61 @@
 
     slots, model = rows.shape
     depth = weight_ref.shape[0]
-    half = depth // 2
     ff = hidden.shape[1]
     lanes = pack.shape[1]
     per_row = model // lanes
     block = in_from.shape[1]
-    wide_step = 2 * lanes
-    steps = model // wide_step
+    quarter = model // RING
+    group = per_row // RING
 
     def columns(i, width):
         return pl.ds(pl.multiple_of(i * width, width), width)
 
-    def pack_column(c, value):
-        pack[pl.ds(c, slots, stride=per_row), :] = value
+    def pack_columns(i, value):
+        for c in range(group):
+            pack[pl.ds(i * group + c, slots, stride=per_row), :] = value[
+                :, c * lanes : (c + 1) * lanes
+            ]
 
     def to_blocks(dst):
+        several = experts // RING
+
         def one(i, carry):
-            dst[i] = pack[columns(i, block), :].astype(dst.dtype)
+            value = pack[columns(i, several * block), :].astype(dst.dtype)
+            dst[pl.ds(i * several, several)] = value.reshape((several, block, lanes))
             return carry
 
-        lax.fori_loop(0, experts, one, 0)
-
-    def to_rows(src):
+        lax.fori_loop(0, RING, one, 0)
+
+    def to_rows(src, dst):
+        several = experts // RING
+
         def one(i, carry):
-            pack[columns(i, block), :] = src[i].astype(jnp.float32)
+            value = src[pl.ds(i * several, several)].astype(jnp.float32)
+            pack[columns(i, several * block), :] = value.reshape((several * block, lanes))
             return carry
 
-        def other(c, carry):
-            rows[:, columns(c, lanes)] = pack[pl.ds(c, slots, stride=per_row), :].astype(rows.dtype)
+        def other(i, carry):
+            for c in range(group):
+                value = pack[pl.ds(i * group + c, slots, stride=per_row), :]
+                dst[:, columns(i * group + c, lanes)] = value.astype(dst.dtype)
             return carry
 
-        lax.fori_loop(0, experts, one, 0)
-        lax.fori_loop(0, per_row, other, 0)
-
-    def place_in(c, carry):
-        value = tokens_ref[:, columns(c, lanes)]
-        pack_column(c, jnp.dot(place_ref[...], value, preferred_element_type=jnp.float32))
-        return carry
-
-    def place_up(c, carry):
-        value = gates_ref[...] * cot_ref[:, columns(c, lanes)].astype(jnp.float32)
+        lax.fori_loop(0, RING, one, 0)
+        lax.fori_loop(0, RING, other, 0)
+
+    def place_in(i, carry):
+        value = tokens_ref[:, columns(i, quarter)]
+        pack_columns(i, jnp.dot(place_ref[...], value, preferred_element_type=jnp.float32))
+        return carry
+
+    def place_up(i, carry):
+        value = gates_ref[...] * cot_ref[:, columns(i, quarter)].astype(jnp.float32)
         value = value.astype(cot_ref.dtype)
-        pack_column(c, jnp.dot(place_ref[...], value, preferred_element_type=jnp.float32))
-        return carry
-
-    lax.fori_loop(0, per_row, place_in, 0)
+        pack_columns(i, jnp.dot(place_ref[...], value, preferred_element_type=jnp.float32))
+        return carry
+
+    lax.fori_loop(0, RING, place_in, 0)
     to_blocks(in_from)
     all_here()
 
@@ -228,110 +246,128 @@
         copy.start()
         sent.append(copy)
 
-    def slot(index, first=0, count=depth):
-        return whole.at[pl.ds(pl.multiple_of(index * depth + first, half), count), :]
-
     blocks = [dp, left[0], right[0], ring_z[1][0]]
-
-    def z_copy(i, src, index, part, device):
-        return send(src, slot(index, *part), wz_send.at[i], wz_recv.at[i], device)
-
-    def z_arrival(i, index, part):
-        there = slot(index, *part)
-        send(there, there, wz_send.at[i], wz_recv.at[i], right).wait_recv()
-
+    half = depth // 2
     every, low, high = (0, depth), (0, half), (half, half)
 
-    def spread_weight(k, src):
-        for s in range(1, RING):
-            start(
-                send(
-                    src,
-                    slot(blocks[k]),
-                    wy_send.at[k, s - 1],
-                    wy_recv.at[k, s - 1],
-                    ring_y[s - 1],
+    def gather(src, dst, zs, zr, ys, yr, cs, cr):
+        def slot(index, first=0, count=depth):
+            return dst.at[pl.ds(pl.multiple_of(index * depth + first, half), count), :]
+
+        def z_copy(i, from_ref, index, part, device):
+            return send(from_ref, slot(index, *part), zs.at[i], zr.at[i], device)
+
+        def z_arrival(i, index, part):
+            there = slot(index, *part)
+            send(there, there, zs.at[i], zr.at[i], right).wait_recv()
+
+        def spread_weight(k, from_ref):
+            for s in range(1, RING):
+                start(
+                    send(
+                        from_ref,
+                        slot(blocks[k]),
+                        ys.at[k, s - 1],
+                        yr.at[k, s - 1],
+                        ring_y[s - 1],
+                    )
                 )
-            )
-        start(send(src, slot(blocks[k]), wc_send.at[k, 0], wc_recv.at[k, 0], sibling))
-
-    def pass_on(k):
-        for s in range(1, RING):
-            there = slot(index_of(blocks[k] // (RING * CORES), y + RING - s, core))
-            send(there, there, wy_send.at[k, s - 1], wy_recv.at[k, s - 1], sibling).wait_recv()
-            start(send(there, there, wc_send.at[k, s], wc_recv.at[k, s], sibling))
-
-    own = pltpu.make_async_copy(weight_ref, slot(dp), local_sem)
+            start(send(from_ref, slot(blocks[k]), cs.at[k, 0], cr.at[k, 0], sibling))
+
+        def begin():
+            start(z_copy(0, src, dp, every, right))
+            start(z_copy(1, src, dp, every, left))
+            spread_weight(0, src)
+
+        def neighbours():
+            z_arrival(0, blocks[1], every)
+            start(z_copy(2, slot(blocks[1], *low), blocks[1], low, right))
+            spread_weight(1, slot(blocks[1]))
+            z_arrival(1, blocks[2], every)
+            start(z_copy(3, slot(blocks[2], *high), blocks[2], high, left))
+            spread_weight(2, slot(blocks[2]))
+
+        def opposite():
+            z_arrival(2, blocks[3], low)
+            z_arrival(3, blocks[3], high)
+            spread_weight(3, slot(blocks[3]))
+
+        def pass_on(k):
+            for s in range(1, RING):
+                there = slot(index_of(blocks[k] // (RING * CORES), y + RING - s, core))
+                send(there, there, ys.at[k, s - 1], yr.at[k, s - 1], sibling).wait_recv()
+                start(send(there, there, cs.at[k, s], cr.at[k, s], sibling))
+
+        def complete(k):
+            for s in range(RING):
+                there = slot(index_of(blocks[k] // (RING * CORES), y + RING - s, 1 - core))
+                send(there, there, cs.at[k, s], cr.at[k, s], sibling).wait_recv()
+
+        own = pltpu.make_async_copy(src, slot(dp), local_sem.at[0 if dst is whole else 1])
+        return own, begin, neighbours, opposite, pass_on, complete
+
+    gate_up = gather(
+        weight_ref.at[:, pl.ds(0, 2 * ff)],
+        whole,
+        wz_send,
+        wz_recv,
+        wy_send,
+        wy_recv,
+        wc_send,
+        wc_recv,
+    )
+    down = gather(
+        weight_ref.at[:, pl.ds(2 * ff, ff)],
+        whole_down,
+        dz_send,
+        dz_recv,
+        dy_send,
+        dy_recv,
+        dc_send,
+        dc_recv,
+    )
+    own, begin, neighbours, opposite, pass_on, complete = gate_up
+    begin()
+    in_there, in_left = exchange(experts, dp, ex, in_from, in_to, in_send, in_recv)
     own.start()
-    start(z_copy(0, weight_ref, dp, every, right))
-    start(z_copy(1, weight_ref, dp, every, left))
-    in_there, in_left = exchange(experts, dp, ex, in_from, in_to, in_send, in_recv)
-    spread_weight(0, weight_ref)
     in_to[ex] = in_from[ex]
-    lax.fori_loop(0, per_row, place_up, 0)
+    lax.fori_loop(0, RING, place_up, 0)
     to_blocks(up_from)
     up_there, up_left = exchange(experts, dp, ex, up_from, up_to, up_send, up_recv)
     up_to[ex] = up_from[ex]
-    z_arrival(0, blocks[1], every)
-    start(z_copy(2, slot(blocks[1], *low), blocks[1], low, right))
-    spread_weight(1, slot(blocks[1]))
-    z_arrival(1, blocks[2], every)
-    start(z_copy(3, slot(blocks[2], *high), blocks[2], high, left))
-    spread_weight(2, slot(blocks[2]))
+    both[...] = jnp.zeros_like(both)
+    neighbours()
     pass_on(0)
-    z_arrival(2, blocks[3], low)
-    z_arrival(3, blocks[3], high)
-    spread_weight(3, slot(blocks[3]))
     in_there()
-    to_rows(in_to)
+    to_rows(in_to, rows)
+    own.wait()
+
+    def multiply(k):
+        complete(k)
+        part = columns(blocks[k] // (RING * CORES), quarter)
+        both[...] += jnp.dot(rows[:, part], whole[part, :], preferred_element_type=jnp.float32)
+
+    opposite()
     pass_on(1)
     pass_on(2)
+    multiply(0)
+    multiply(1)
+    multiply(2)
     pass_on(3)
-    for k in range(RING):
-        for s in range(RING):
-            there = slot(index_of(blocks[k] // (RING * CORES), y + RING - s, 1 - core))
-            send(there, there, wc_send.at[k, s], wc_recv.at[k, s], sibling).wait_recv()
-    own.wait()
-
-    both[...] = jnp.zeros_like(both)
-
-    def gate_up(i, carry):
-        both[...] += jnp.dot(
-            rows[:, columns(i, wide_step)],
-            whole[columns(i, wide_step), pl.ds(0, 2 * ff)],
-            preferred_element_type=jnp.float32,
-        )
-        return carry
-
-    lax.fori_loop(0, steps, gate_up, 0)
+    up_there()
+    to_rows(up_to, rows_up)
+    multiply(3)
+    own, begin, neighbours, opposite, pass_on, complete = down
+    begin()
+    own.start()
     hidden[...] = (silu_value(both[:, :ff]) * both[:, ff:]).astype(hidden.dtype)
 
-    def down(i, carry):
-        value = lax.dot_general(
-            hidden[...],
-            whole[columns(i, wide_step), pl.ds(2 * ff, ff)],
-            (((1,), (1,)), ((), ())),
-            preferred_element_type=jnp.float32,
-        )
-        pack_column(2 * i, value[:, :lanes])
-        pack_column(2 * i + 1, value[:, lanes:])
-        return carry
-
-    lax.fori_loop(0, steps, down, 0)
-    to_blocks(out_from)
-    out_there, out_left = exchange(experts, dp, ex, out_from, out_to, out_send, out_recv)
-    out_to[ex] = out_from[ex]
-
-    up_there()
-    to_rows(up_to)
-    pairs = wide_step // (CORES * depth)
-
     def grad(i, carry):
-        value = contract_rows(rows[:, columns(i, wide_step)], hidden[...]).astype(partial.dtype)
-        partial[pl.ds(i * pairs, pairs)] = value.reshape((pairs, CORES, depth, ff))
-        return carry
-
-    lax.fori_loop(0, steps, grad, 0)
+        value = contract_rows(rows_up[:, columns(i, quarter)], hidden[...]).astype(partial.dtype)
+        partial[pl.ds(i * RING, RING)] = value.reshape((RING, CORES, depth, ff))
+        return carry
+
+    lax.fori_loop(0, RING, grad, 0)
     to_core = send(partial.at[:, 1 - core], c_buf, c_send, c_recv, sibling)
     to_core.start()
     to_core.wait()
@@ -356,6 +392,8 @@
     ]
     for copy in y_copies:
         copy.start()
+    neighbours()
+    pass_on(0)
     for copy in y_copies:
         copy.wait()
 
@@ -379,6 +417,27 @@
     ]
     for copy in z_copies:
         copy.start()
+    opposite()
+    for k in range(1, RING):
+        pass_on(k)
+    for k in range(RING):
+        complete(k)
+    own.wait()
+
+    def outputs(i, carry):
+        value = lax.dot_general(
+            hidden[...],
+            whole_down[columns(i, quarter), :],
+            (((1,), (1,)), ((), ())),
+            preferred_element_type=jnp.float32,
+        )
+        pack_columns(i, value)
+        return carry
+
+    lax.fori_loop(0, RING, outputs, 0)
+    to_blocks(out_from)
+    out_there, out_left = exchange(experts, dp, ex, out_from, out_to, out_send, out_recv)
+    out_to[ex] = out_from[ex]
     for copy in z_copies:
         copy.wait()
     grads = z_from[z].astype(jnp.float32)
@@ -443,6 +502,20 @@
         lax.fori_loop(1, experts, start, 0)
         arrived[mine] = ordered[ex]
 
+    out_there()
+    to_rows(out_to, rows)
+
+    def combine(i, total):
+        part = columns(i, quarter)
+        value = jnp.dot(pick_ref[...], rows[:, part], preferred_element_type=jnp.float32)
+        combined_ref[:, part] = (gates_ref[...] * value).astype(combined_ref.dtype)
+        return total + cot_ref[:, part].astype(jnp.float32) * value
+
+    total = lax.fori_loop(
+        0, RING, combine, jnp.zeros((tokens_ref.shape[0], quarter), jnp.float32)
+    )
+    gate_grads_ref[...] = jnp.sum(total, axis=1, keepdims=True)
+
     for q in range(pieces):
         there = arrived.at[q]
 
@@ -465,20 +538,6 @@
 
         lax.fori_loop(1, experts, sent, 0)
 
-    out_there()
-    to_rows(out_to)
-
-    def combine(c, total):
-        value = jnp.dot(
-            pick_ref[...], rows[:, columns(c, lanes)], preferred_element_type=jnp.float32
-        )
-        combined_ref[:, columns(c, lanes)] = (gates_ref[...] * value).astype(combined_ref.dtype)
-        return total + cot_ref[:, columns(c, lanes)].astype(jnp.float32) * value
-
-    total = lax.fori_loop(
-        0, per_row, combine, jnp.zeros((tokens_ref.shape[0], lanes), jnp.float32)
-    )
-    gate_grads_ref[...] = jnp.sum(total, axis=1, keepdims=True)
     for copy in sent:
         copy.wait_send()
     in_left()
@@ -512,8 +571,10 @@
         in_specs=[VMEM] * 9 + [pl.BlockSpec(memory_space=pltpu.SMEM)],
         out_specs=[VMEM] * 6,
         scratch_shapes=[
-            sixteen(model, 3 * ff),
+            sixteen(model, 2 * ff),
+            sixteen(model, ff),
             pltpu.VMEM((slots * model // lanes, lanes), jnp.float32),
+            sixteen(slots, model),
             sixteen(slots, model),
             pltpu.VMEM((slots, 2 * ff), jnp.float32),
             sixteen(slots, ff),
@@ -530,12 +591,10 @@
             sixteen(experts, *piece),
             sixteen(experts, *piece),
             sixteen(pieces, *piece),
-            dma,
+            dma((2,)),
         ]
         + [dma((experts,))] * 6
-        + [dma((RING,))] * 2
-        + [dma((RING, RING - 1))] * 2
-        + [dma((RING, RING))] * 2
+        + ([dma((RING,))] * 2 + [dma((RING, RING - 1))] * 2 + [dma((RING, RING))] * 2) * 2
         + [dma] * 2
         + [dma((RING - 1,))] * 4
         + [dma((pieces,)), dma((experts,)), dma((experts,)), dma((pieces,))],

time: 222 us -> 215 us (0.968)
  Pallas kernels: 210 us -> 202 us
    pallas_call x1, Pallas kernels: 210 us -> 202 us  [layer(): pl.pallas_call(functools.partial(layer_kernel, experts), out_shape=[jax.S...]
where the time goes in v4:
time: 215 us; the launch traced here: 212 us
  Pallas kernels  202 us (94%)
  local copies, waits for them, and re-layouts  8.14 us (4%)
    pallas_call x1, Pallas kernels, layer(): pl.pallas_call(functools.partial(layer_kernel, experts), out_shape=[jax.S...  202 us
    unnamed x27, local copies, waits for them, and re-layouts  8.14 us

profile of v4, /device:TPU:24, one launch (start us, length us, event | category | flops | bytes accessed | tf_op | source)
XLA Modules:
  0.0 211.8 jit_solution(9888070663715500614)
XLA Ops:
  0.6 0.0 copy-start.8
  0.6 0.0 copy-start.9
  0.7 0.6 copy-done.8
  1.3 0.0 copy-done.9
  1.3 0.2 select_reduce_fusion.2
  1.5 0.0 copy-start.6
  1.5 0.7 copy-done.6
  2.1 0.0 copy-start.5
  2.1 0.1 fusion.2
  2.2 0.0 copy-start.4
  2.2 0.2 reduce_window_sum.11
  2.4 0.0 copy-start.7
  2.4 0.0 copy-start.2
  2.4 0.2 select_reduce_fusion.1
  2.6 0.0 copy-start.3
  2.7 0.1 fusion.pick_ref
  2.8 0.3 copy-done.7
  3.1 0.1 copy.18.gates_ref
  3.2 0.0 copy-done.5
  3.2 0.0 copy-done.4
  3.2 0.2 copy-done.2
  3.4 0.2 copy-done.3
  3.6 0.0 copy-start
  3.6 1.0 copy-done
  4.6 0.0 copy-start.1
  4.6 1.0 copy-done.1
  5.6 202.2 %layer.1 = (bf16[128,2048]{1,0:T(8,128)(2,1)S(1)}, f32[128,1]{1,0:T(8,128)S(1)}, f32[64,384]{1,0:T(8,128)S(1)}, f32[64,384]{1,0:T(8,128)S(1)}, f32[64,384]{1,0:T(8,128)S(1)}, /*index=5*/f32[64,384]{1,0:T(8,128)S(1)}) custom-call(bf16[160,128]{1,0:T(8,128)(2,1)S(1)} %fusion.1.place_ref, bf16[128,160]{1,0:T(8,128)(2,1)S(1)} %fusion.pick_ref, ...), custom_call_target="tpu_custom_call" | custom-call | tf_op jit(solution)/shard_map/layer/pallas_call | solution.py:564
  207.8 0.6 copy.19
  208.4 0.8 copy.25
  209.2 0.6 copy.26
  209.8 0.6 copy.27
  210.5 0.6 copy.28
  211.1 0.6 copy.29
  (2 shorter events, 0.0 us)
Async XLA Ops:
  0.6 0.7 copy-start.8
  0.6 0.7 copy-start.9
  1.5 0.7 copy-start.6
  2.1 1.0 copy-start.5
  2.2 1.0 copy-start.4
  2.4 0.7 copy-start.7
  2.4 0.9 copy-start.2
  2.6 0.9 copy-start.3
  3.6 1.0 copy-start
  4.6 1.0 copy-start.1

commit v5 on v4

--- a/solution.py
+++ b/solution.py
@@ -16,6 +16,8 @@
 VMEM = pl.BlockSpec(memory_space=pltpu.VMEM)
 RING = 4
 CORES = 2
+HALVES = 2
+NODES = RING * HALVES
 
 
 def silu_value(values):
@@ -63,11 +65,17 @@
     return lambda: pl.semaphore_wait(barrier, len(devices) + experts - 1)
 
 
-def exchange(experts, dp, ex, src, dst, send_sems, recv_sems):
+def exchange(hosts, dp, ex, src, dst, send_sems, recv_sems):
+    me, first = ex % hosts, ex - ex % hosts
+
     def copy(step):
-        target = (ex + step) % experts
+        target = (me + step) % hosts
         return send(
-            src.at[target], dst.at[ex], send_sems.at[target], recv_sems.at[ex], (dp, target)
+            src.at[:, target],
+            dst.at[:, me],
+            send_sems.at[target],
+            recv_sems.at[me],
+            (dp, first + target),
         )
 
     def start(step, carry):
@@ -75,19 +83,23 @@
         return carry
 
     def arrival(step, carry):
-        other = (ex + step) % experts
-        there = dst.at[other]
-        send(there, there, send_sems.at[other], recv_sems.at[other], (dp, other)).wait_recv()
+        other = (me + step) % hosts
+        there = dst.at[:, other]
+        send(
+            there, there, send_sems.at[other], recv_sems.at[other], (dp, first + other)
+        ).wait_recv()
         return carry
 
     def departure(step, carry):
         copy(step).wait_send()
         return carry
 
-    lax.fori_loop(1, experts, start, 0)
+    lax.fori_loop(1, hosts, start, 0)
+    for half in range(HALVES):
+        dst[half, me] = src[half, me]
     return (
-        lambda: lax.fori_loop(1, experts, arrival, 0),
-        lambda: lax.fori_loop(1, experts, departure, 0),
+        lambda: lax.fori_loop(1, hosts, arrival, 0),
+        lambda: lax.fori_loop(1, hosts, departure, 0),
     )
 
 
@@ -137,6 +149,7 @@
     c_buf,
     y_from,
     y_buf,
+    z_own,
     z_from,
     z_buf,
     state,
@@ -176,16 +189,24 @@
     dp, ex, z, y, core = place()
     sibling = (index_of(z, y, 1 - core), ex)
     ring_y = [(index_of(z, y + s, core), ex) for s in range(1, RING)]
-    ring_z = [(index_of(z + s, y, core), ex) for s in range(1, RING)]
-    right, left = ring_z[0], ring_z[2]
-    all_here = greet([sibling] + ring_y + ring_z, experts, dp, ex)
+    hosts = experts // HALVES
+    node = z * HALVES + ex // hosts
+
+    def at_node(step):
+        other = (node + step + NODES) % NODES
+        return (index_of(other // HALVES, y, core), other % HALVES * hosts + ex % hosts)
+
+    right, left = at_node(1), at_node(-1)
+    outer = at_node(2 * (ex // hosts) - 1)
+    all_here = greet([sibling, outer] + ring_y, experts, dp, ex)
 
     slots, model = rows.shape
     depth = weight_ref.shape[0]
     ff = hidden.shape[1]
     lanes = pack.shape[1]
     per_row = model // lanes
-    block = in_from.shape[1]
+    block = in_from.shape[2]
+    part_rows = slots // HALVES
     quarter = model // RING
     group = per_row // RING
 
@@ -199,22 +220,16 @@
             ]
 
     def to_blocks(dst):
-        several = experts // RING
-
-        def one(i, carry):
-            value = pack[columns(i, several * block), :].astype(dst.dtype)
-            dst[pl.ds(i * several, several)] = value.reshape((several, block, lanes))
-            return carry
-
-        lax.fori_loop(0, RING, one, 0)
+        for half in range(HALVES):
+            value = pack[pl.ds(half * hosts * block, hosts * block), :].astype(dst.dtype)
+            dst[half] = value.reshape((hosts, block, lanes))
 
     def to_rows(src, dst):
-        several = experts // RING
-
-        def one(i, carry):
-            value = src[pl.ds(i * several, several)].astype(jnp.float32)
-            pack[columns(i, several * block), :] = value.reshape((several * block, lanes))
-            return carry
+        for half in range(HALVES):
+            value = src[half].astype(jnp.float32)
+            pack[pl.ds(half * hosts * block, hosts * block), :] = value.reshape(
+                (hosts * block, lanes)
+            )
 
         def other(i, carry):
             for c in range(group):
@@ -222,7 +237,6 @@
                 dst[:, columns(i * group + c, lanes)] = value.astype(dst.dtype)
             return carry
 
-        lax.fori_loop(0, RING, one, 0)
         lax.fori_loop(0, RING, other, 0)
 
     def place_in(i, carry):
@@ -246,65 +260,63 @@
         copy.start()
         sent.append(copy)
 
-    blocks = [dp, left[0], right[0], ring_z[1][0]]
+    nodes = [(node + step + NODES) % NODES for step in (0, -1, 1, -2, 2, -3, 3, 4)]
     half = depth // 2
     every, low, high = (0, depth), (0, half), (half, half)
 
     def gather(src, dst, zs, zr, ys, yr, cs, cr):
-        def slot(index, first=0, count=depth):
-            return dst.at[pl.ds(pl.multiple_of(index * depth + first, half), count), :]
-
-        def z_copy(i, from_ref, index, part, device):
-            return send(from_ref, slot(index, *part), zs.at[i], zr.at[i], device)
-
-        def z_arrival(i, index, part):
-            there = slot(index, *part)
+        def slot(k, first=0, count=depth, y=y, core=core):
+            row = index_of(nodes[k] // HALVES, y, core) * depth + first
+            return dst.at[nodes[k] % HALVES, pl.ds(pl.multiple_of(row, half), count), :]
+
+        def z_copy(i, from_ref, k, part, device):
+            return send(from_ref, slot(k, *part), zs.at[i], zr.at[i], device)
+
+        def z_arrival(i, k, part=every):
+            there = slot(k, *part)
             send(there, there, zs.at[i], zr.at[i], right).wait_recv()
 
         def spread_weight(k, from_ref):
             for s in range(1, RING):
                 start(
-                    send(
-                        from_ref,
-                        slot(blocks[k]),
-                        ys.at[k, s - 1],
-                        yr.at[k, s - 1],
-                        ring_y[s - 1],
-                    )
+                    send(from_ref, slot(k), ys.at[k, s - 1], yr.at[k, s - 1], ring_y[s - 1])
                 )
-            start(send(from_ref, slot(blocks[k]), cs.at[k, 0], cr.at[k, 0], sibling))
+            start(send(from_ref, slot(k), cs.at[k, 0], cr.at[k, 0], sibling))
 
         def begin():
-            start(z_copy(0, src, dp, every, right))
-            start(z_copy(1, src, dp, every, left))
+            start(z_copy(0, src, 0, every, right))
+            start(z_copy(1, src, 0, every, left))
             spread_weight(0, src)
 
-        def neighbours():
-            z_arrival(0, blocks[1], every)
-            start(z_copy(2, slot(blocks[1], *low), blocks[1], low, right))
-            spread_weight(1, slot(blocks[1]))
-            z_arrival(1, blocks[2], every)
-            start(z_copy(3, slot(blocks[2], *high), blocks[2], high, left))
-            spread_weight(2, slot(blocks[2]))
+        def arrive(step):
+            from_left, from_right = 2 * step - 1, 2 * step
+            part = every if step < 3 else low
+            z_arrival(2 * step - 2, from_left)
+            start(z_copy(2 * step, slot(from_left, *part), from_left, part, right))
+            part = every if step < 3 else high
+            z_arrival(2 * step - 1, from_right)
+            start(z_copy(2 * step + 1, slot(from_right, *part), from_right, part, left))
+            spread_weight(from_left, slot(from_left))
+            spread_weight(from_right, slot(from_right))
 
         def opposite():
-            z_arrival(2, blocks[3], low)
-            z_arrival(3, blocks[3], high)
-            spread_weight(3, slot(blocks[3]))
+            z_arrival(6, 7, low)
+            z_arrival(7, 7, high)
+            spread_weight(7, slot(7))
 
         def pass_on(k):
             for s in range(1, RING):
-                there = slot(index_of(blocks[k] // (RING * CORES), y + RING - s, core))
+                there = slot(k, y=y + RING - s)
                 send(there, there, ys.at[k, s - 1], yr.at[k, s - 1], sibling).wait_recv()
                 start(send(there, there, cs.at[k, s], cr.at[k, s], sibling))
 
         def complete(k):
             for s in range(RING):
-                there = slot(index_of(blocks[k] // (RING * CORES), y + RING - s, 1 - core))
+                there = slot(k, y=y + RING - s, core=1 - core)
                 send(there, there, cs.at[k, s], cr.at[k, s], sibling).wait_recv()
 
-        own = pltpu.make_async_copy(src, slot(dp), local_sem.at[0 if dst is whole else 1])
-        return own, begin, neighbours, opposite, pass_on, complete
+        own = pltpu.make_async_copy(src, slot(0), local_sem.at[0 if dst is whole else 1])
+        return own, begin, arrive, opposite, pass_on, complete
 
     gate_up = gather(
         weight_ref.at[:, pl.ds(0, 2 * ff)],
@@ -326,57 +338,76 @@
         dc_send,
         dc_recv,
     )
-    own, begin, neighbours, opposite, pass_on, complete = gate_up
+    own, begin, arrive, opposite, pass_on, complete = gate_up
     begin()
-    in_there, in_left = exchange(experts, dp, ex, in_from, in_to, in_send, in_recv)
+    in_there, in_left = exchange(hosts, dp, ex, in_from, in_to, in_send, in_recv)
     own.start()
-    in_to[ex] = in_from[ex]
     lax.fori_loop(0, RING, place_up, 0)
     to_blocks(up_from)
-    up_there, up_left = exchange(experts, dp, ex, up_from, up_to, up_send, up_recv)
-    up_to[ex] = up_from[ex]
+    up_there, up_left = exchange(hosts, dp, ex, up_from, up_to, up_send, up_recv)
     both[...] = jnp.zeros_like(both)
-    neighbours()
+
+    def rows_of(half):
+        return pl.ds(pl.multiple_of(half * part_rows, part_rows), part_rows)
+
+    def multiply(k):
+        complete(k)
+        half, part = nodes[k] % HALVES, columns(nodes[k] // HALVES, quarter)
+        these = rows_of(half)
+        both[these, :] += jnp.dot(
+            rows[these, part], whole[half, part, :], preferred_element_type=jnp.float32
+        )
+
+    arrive(1)
     pass_on(0)
+    arrive(2)
+    pass_on(1)
+    pass_on(2)
     in_there()
     to_rows(in_to, rows)
     own.wait()
-
-    def multiply(k):
-        complete(k)
-        part = columns(blocks[k] // (RING * CORES), quarter)
-        both[...] += jnp.dot(rows[:, part], whole[part, :], preferred_element_type=jnp.float32)
-
-    opposite()
-    pass_on(1)
-    pass_on(2)
+    arrive(3)
+    pass_on(3)
+    pass_on(4)
     multiply(0)
     multiply(1)
     multiply(2)
-    pass_on(3)
+    opposite()
+    pass_on(5)
+    pass_on(6)
+    multiply(3)
+    multiply(4)
+    multiply(5)
+    multiply(6)
+    pass_on(7)
     up_there()
     to_rows(up_to, rows_up)
-    multiply(3)
-    own, begin, neighbours, opposite, pass_on, complete = down
+    multiply(7)
+    own, begin, arrive, opposite, pass_on, complete = down
     begin()
     own.start()
     hidden[...] = (silu_value(both[:, :ff]) * both[:, ff:]).astype(hidden.dtype)
 
     def grad(i, carry):
-        value = contract_rows(rows_up[:, columns(i, quarter)], hidden[...]).astype(partial.dtype)
-        partial[pl.ds(i * RING, RING)] = value.reshape((RING, CORES, depth, ff))
+        for half in range(HALVES):
+            these = pl.ds(half * part_rows, part_rows)
+            value = contract_rows(rows_up[these, columns(i, quarter)], hidden[these, :])
+            partial[half, pl.ds(i * RING, RING)] = value.astype(partial.dtype).reshape(
+                (RING, CORES, depth, ff)
+            )
         return carry
 
     lax.fori_loop(0, RING, grad, 0)
-    to_core = send(partial.at[:, 1 - core], c_buf, c_send, c_recv, sibling)
+    to_core = send(partial.at[:, :, 1 - core], c_buf, c_send, c_recv, sibling)
     to_core.start()
     to_core.wait()
 
     def pair(i, carry):
         at, row = i // RING, i % RING
-        y_from[row, at] = (
-            partial[i, core].astype(jnp.float32) + c_buf[i].astype(jnp.float32)
-        ).astype(y_from.dtype)
+        for half in range(HALVES):
+            y_from[row, half, at] = (
+                partial[half, i, core].astype(jnp.float32) + c_buf[half, i].astype(jnp.float32)
+            ).astype(y_from.dtype)
         return carry
 
     lax.fori_loop(0, RING * RING, pair, 0)
@@ -392,57 +423,74 @@
     ]
     for copy in y_copies:
         copy.start()
-    neighbours()
+    arrive(1)
     pass_on(0)
     for copy in y_copies:
         copy.wait()
 
     def quad(i, carry):
-        total = y_from[y, i].astype(jnp.float32)
-        for s in range(RING - 1):
-            total += y_buf[s, i].astype(jnp.float32)
-        z_from[i] = total.astype(z_from.dtype)
+        for part in range(HALVES):
+            total = y_from[y, part, i].astype(jnp.float32)
+            for s in range(RING - 1):
+                total += y_buf[s, part, i].astype(jnp.float32)
+            z_own[i * HALVES + part] = total
         return carry
 
     lax.fori_loop(0, RING, quad, 0)
-    z_copies = [
-        send(
-            z_from.at[(z + s) % RING],
-            z_buf.at[s - 1],
-            z_send.at[s - 1],
-            z_recv.at[s - 1],
-            ring_z[s - 1],
+
+    def mine(step):
+        return z_own[(node + step + NODES) % NODES]
+
+    def ring_copy(step, way):
+        rows_sent = pl.ds(way * half, half) if step == 0 else pl.ds(0, depth)
+        return send(
+            z_from.at[way, step, rows_sent],
+            z_buf.at[way, step, rows_sent],
+            z_send.at[way, step],
+            z_recv.at[way, step],
+            (right, left)[way],
         )
-        for s in range(1, RING)
-    ]
-    for copy in z_copies:
-        copy.start()
+
+    def ring_step(step):
+        for way in range(2):
+            total = mine((NODES // 2 - step) * (1 - 2 * way))
+            if step == 0:
+                cut = slice(way * half, way * half + half)
+                z_from[way, step, cut, :] = total[cut].astype(z_from.dtype)
+            elif step == 1:
+                ring_copy(0, way).wait_recv()
+                here, there = (0, half) if way == 0 else (half, 0)
+                z_from[way, step, here : here + half, :] = (
+                    total[here : here + half]
+                    + z_buf[way, 0, here : here + half, :].astype(jnp.float32)
+                ).astype(z_from.dtype)
+                z_from[way, step, there : there + half, :] = total[there : there + half].astype(
+                    z_from.dtype
+                )
+            else:
+                ring_copy(step - 1, way).wait_recv()
+                z_from[way, step] = (total + z_buf[way, step - 1].astype(jnp.float32)).astype(
+                    z_from.dtype
+                )
+            ring_copy(step, way).start()
+
+    last = NODES // 2 - 1
+    ring_step(0)
+    arrive(2)
+    ring_step(1)
+    pass_on(1)
+    pass_on(2)
+    ring_step(2)
+    arrive(3)
+    pass_on(3)
+    pass_on(4)
+    ring_step(3)
     opposite()
-    for k in range(1, RING):
-        pass_on(k)
-    for k in range(RING):
-        complete(k)
-    own.wait()
-
-    def outputs(i, carry):
-        value = lax.dot_general(
-            hidden[...],
-            whole_down[columns(i, quarter), :],
-            (((1,), (1,)), ((), ())),
-            preferred_element_type=jnp.float32,
-        )
-        pack_columns(i, value)
-        return carry
-
-    lax.fori_loop(0, RING, outputs, 0)
-    to_blocks(out_from)
-    out_there, out_left = exchange(experts, dp, ex, out_from, out_to, out_send, out_recv)
-    out_to[ex] = out_from[ex]
-    for copy in z_copies:
-        copy.wait()
-    grads = z_from[z].astype(jnp.float32)
-    for s in range(RING - 1):
-        grads += z_buf[s].astype(jnp.float32)
+    pass_on(5)
+    pass_on(6)
+    for way in range(2):
+        ring_copy(last, way).wait_recv()
+    grads = mine(0) + z_buf[0, last].astype(jnp.float32) + z_buf[1, last].astype(jnp.float32)
     grads_ref[...] = grads
     first = beta_first * first_ref[...] + (1.0 - beta_first) * grads
     second = beta_second * second_ref[...] + (1.0 - beta_second) * grads * grads
@@ -460,7 +508,7 @@
             row, column = q // across * tall, q % across * wide
             state[q, i] = value[row : row + tall, column : column + wide]
 
-    is_middle, mine = middle_of(ex, core)
+    is_middle, held = middle_of(ex, core)
 
     def spread_copy(q):
         return send(
@@ -476,12 +524,36 @@
     def order_copy(step):
         target = (ex + step) % experts
         return send(
-            ordered.at[target], arrived.at[mine], t_send.at[target], t_recv.at[mine], (dp, target)
+            ordered.at[target], arrived.at[held], t_send.at[target], t_recv.at[held], (dp, target)
         )
+
+    pass_on(7)
+    for k in range(NODES):
+        complete(k)
+    own.wait()
+
+    def outputs(i, carry):
+        for part in range(HALVES):
+            value = lax.dot_general(
+                hidden[pl.ds(part * part_rows, part_rows), :],
+                whole_down[part, columns(i, quarter), :],
+                (((1,), (1,)), ((), ())),
+                preferred_element_type=jnp.float32,
+            )
+            for c in range(group):
+                first_row = part * part_rows * per_row + i * group + c
+                pack[pl.ds(first_row, part_rows, stride=per_row), :] = value[
+                    :, c * lanes : (c + 1) * lanes
+                ]
+        return carry
+
+    lax.fori_loop(0, RING, outputs, 0)
+    to_blocks(out_from)
+    out_there, out_left = exchange(hosts, dp, ex, out_from, out_to, out_send, out_recv)
 
     @pl.when(is_middle)
     def _():
-        spread[ex] = state[mine]
+        spread[ex] = state[held]
 
         def landed(step, carry):
             other = (ex + step) % experts
@@ -500,7 +572,7 @@
         lax.fori_loop(1, experts, landed, 0)
         lax.fori_loop(0, experts, pick, 0)
         lax.fori_loop(1, experts, start, 0)
-        arrived[mine] = ordered[ex]
+        arrived[held] = ordered[ex]
 
     out_there()
     to_rows(out_to, rows)
@@ -540,6 +612,9 @@
 
     for copy in sent:
         copy.wait_send()
+    for step in range(last + 1):
+        for way in range(2):
+            ring_copy(step, way).wait_send()
     in_left()
     up_left()
     out_left()
@@ -553,7 +628,8 @@
     dma = pltpu.SemaphoreType.DMA
     kind = tokens.dtype
     lanes = 128
-    packed = (experts, slots * model // lanes // experts, lanes)
+    hosts = experts // HALVES
+    packed = (HALVES, hosts, slots * model // lanes // experts, lanes)
     block = (depth, ff)
     piece = (3, 16, 128)
     pieces = depth * ff // (16 * 128)
@@ -571,8 +647,8 @@
         in_specs=[VMEM] * 9 + [pl.BlockSpec(memory_space=pltpu.SMEM)],
         out_specs=[VMEM] * 6,
         scratch_shapes=[
-            sixteen(model, 2 * ff),
-            sixteen(model, ff),
+            sixteen(HALVES, model, 2 * ff),
+            sixteen(HALVES, model, ff),
             pltpu.VMEM((slots * model // lanes, lanes), jnp.float32),
             sixteen(slots, model),
             sixteen(slots, model),
@@ -581,25 +657,27 @@
         ]
         + [sixteen(*packed)] * 6
         + [
-            sixteen(RING * RING, CORES, *block),
-            sixteen(RING * RING, *block),
-            sixteen(RING, RING, *block),
-            sixteen(RING - 1, RING, *block),
-            sixteen(RING, *block),
-            sixteen(RING - 1, *block),
+            sixteen(HALVES, RING * RING, CORES, *block),
+            sixteen(HALVES, RING * RING, *block),
+            sixteen(RING, HALVES, RING, *block),
+            sixteen(RING - 1, HALVES, RING, *block),
+            pltpu.VMEM((NODES,) + block, jnp.float32),
+            sixteen(2, NODES // 2, *block),
+            sixteen(2, NODES // 2, *block),
             sixteen(pieces, *piece),
             sixteen(experts, *piece),
             sixteen(experts, *piece),
             sixteen(pieces, *piece),
             dma((2,)),
         ]
-        + [dma((experts,))] * 6
-        + ([dma((RING,))] * 2 + [dma((RING, RING - 1))] * 2 + [dma((RING, RING))] * 2) * 2
+        + [dma((hosts,))] * 6
+        + ([dma((NODES,))] * 2 + [dma((NODES, RING - 1))] * 2 + [dma((NODES, RING))] * 2) * 2
         + [dma] * 2
-        + [dma((RING - 1,))] * 4
+        + [dma((RING - 1,))] * 2
+        + [dma((2, NODES // 2))] * 2
         + [dma((pieces,)), dma((experts,)), dma((experts,)), dma((pieces,))],
         compiler_params=pltpu.CompilerParams(
-            collective_id=0, has_side_effects=True, vmem_limit_bytes=40 * 1024 * 1024
+            collective_id=0, has_side_effects=True, vmem_limit_bytes=48 * 1024 * 1024
         ),
         name="layer",
     )(place_slots, place_slots.T, gates, tokens, cotangent, weight, *state, source)

time: 215 us -> 195 us (0.907)
  the two profiles are of different devices: /device:TPU:24 before, /device:TPU:2 now
where the time goes in v5:
time: 195 us
  Pallas kernels  185 us (95%)
  local copies, waits for them, and re-layouts  8.14 us (4%)
    pallas_call x1, Pallas kernels, layer(): pl.pallas_call(functools.partial(layer_kernel, experts), out_shape=[jax.S...  185 us
    unnamed x27, local copies, waits for them, and re-layouts  8.14 us

profile of v5, /device:TPU:2, one launch (start us, length us, event | category | flops | bytes accessed | tf_op | source)
XLA Modules:
  0.0 194.8 jit_solution(17925795427692112752)
XLA Ops:
  0.6 0.0 copy-start.8
  0.6 0.0 copy-start.9
  0.7 0.6 copy-done.8
  1.3 0.0 copy-done.9
  1.3 0.2 select_reduce_fusion.2
  1.5 0.0 copy-start.6
  1.5 0.7 copy-done.6
  2.1 0.0 copy-start.5
  2.1 0.1 fusion.2
  2.2 0.0 copy-start.4
  2.2 0.2 reduce_window_sum.11
  2.4 0.0 copy-start.7
  2.4 0.0 copy-start.2
  2.4 0.2 select_reduce_fusion.1
  2.6 0.0 copy-start.3
  2.7 0.1 fusion.pick_ref
  2.8 0.3 copy-done.7
  3.1 0.1 copy.18.gates_ref
  3.2 0.0 copy-done.5
  3.2 0.0 copy-done.4
  3.2 0.2 copy-done.2
  3.4 0.2 copy-done.3
  3.6 0.0 copy-start
  3.6 1.0 copy-done
  4.6 0.0 copy-start.1
  4.6 1.0 copy-done.1
  5.6 185.2 %layer.1 = (bf16[128,2048]{1,0:T(8,128)(2,1)S(1)}, f32[128,1]{1,0:T(8,128)S(1)}, f32[64,384]{1,0:T(8,128)S(1)}, f32[64,384]{1,0:T(8,128)S(1)}, f32[64,384]{1,0:T(8,128)S(1)}, /*index=5*/f32[64,384]{1,0:T(8,128)S(1)}) custom-call(bf16[160,128]{1,0:T(8,128)(2,1)S(1)} %fusion.1.place_ref, bf16[128,160]{1,0:T(8,128)(2,1)S(1)} %fusion.pick_ref, ...), custom_call_target="tpu_custom_call" | custom-call | tf_op jit(solution)/shard_map/layer/pallas_call | solution.py:640
  190.8 0.6 copy.19
  191.4 0.8 copy.25
  192.2 0.6 copy.26
  192.9 0.6 copy.27
  193.5 0.6 copy.28
  194.1 0.6 copy.29
  (2 shorter events, 0.0 us)
Async XLA Ops:
  0.6 0.7 copy-start.8
  0.6 0.7 copy-start.9
  1.5 0.7 copy-start.6
  2.1 1.0 copy-start.5
  2.2 1.0 copy-start.4
  2.4 0.7 copy-start.7
  2.4 0.9 copy-start.2
  2.6 0.9 copy-start.3
  3.6 1.0 copy-start
  4.6 1.0 copy-start.1

commit v6 on v5

--- a/solution.py
+++ b/solution.py
@@ -286,6 +286,8 @@
         def begin():
             start(z_copy(0, src, 0, every, right))
             start(z_copy(1, src, 0, every, left))
+
+        def begin_across():
             spread_weight(0, src)
 
         def arrive(step):
@@ -316,7 +318,7 @@
                 send(there, there, cs.at[k, s], cr.at[k, s], sibling).wait_recv()
 
         own = pltpu.make_async_copy(src, slot(0), local_sem.at[0 if dst is whole else 1])
-        return own, begin, arrive, opposite, pass_on, complete
+        return own, begin, begin_across, arrive, opposite, pass_on, complete
 
     gate_up = gather(
         weight_ref.at[:, pl.ds(0, 2 * ff)],
@@ -338,13 +340,13 @@
         dc_send,
         dc_recv,
     )
-    own, begin, arrive, opposite, pass_on, complete = gate_up
+    own, begin, begin_across, arrive, opposite, pass_on, complete = gate_up
     begin()
+    begin_across()
     in_there, in_left = exchange(hosts, dp, ex, in_from, in_to, in_send, in_recv)
     own.start()
     lax.fori_loop(0, RING, place_up, 0)
     to_blocks(up_from)
-    up_there, up_left = exchange(hosts, dp, ex, up_from, up_to, up_send, up_recv)
     both[...] = jnp.zeros_like(both)
 
     def rows_of(half):
@@ -359,6 +361,7 @@
         )
 
     arrive(1)
+    up_there, up_left = exchange(hosts, dp, ex, up_from, up_to, up_send, up_recv)
     pass_on(0)
     arrive(2)
     pass_on(1)
@@ -373,6 +376,8 @@
     multiply(1)
     multiply(2)
     opposite()
+    begin_down = down[1]
+    begin_down()
     pass_on(5)
     pass_on(6)
     multiply(3)
@@ -383,8 +388,8 @@
     up_there()
     to_rows(up_to, rows_up)
     multiply(7)
-    own, begin, arrive, opposite, pass_on, complete = down
-    begin()
+    own, _, begin_across, arrive, opposite, pass_on, complete = down
+    begin_across()
     own.start()
     hidden[...] = (silu_value(both[:, :ff]) * both[:, ff:]).astype(hidden.dtype)
 
@@ -411,32 +416,30 @@
         return carry
 
     lax.fori_loop(0, RING * RING, pair, 0)
-    y_copies = [
-        send(
-            y_from.at[(y + s) % RING],
-            y_buf.at[s - 1],
-            y_send.at[s - 1],
-            y_recv.at[s - 1],
+    order = (4, 3, -3, 2, -2, 1, -1, 0)
+    targets = [(node + step + NODES) % NODES for step in order]
+
+    def y_copy(k, s):
+        at = (targets[k] % HALVES, targets[k] // HALVES)
+        return send(
+            y_from.at[(y + s) % RING, at[0], at[1]],
+            y_buf.at[s - 1, at[0], at[1]],
+            y_send.at[k, s - 1],
+            y_recv.at[k, s - 1],
             ring_y[s - 1],
         )
-        for s in range(1, RING)
-    ]
-    for copy in y_copies:
-        copy.start()
-    arrive(1)
-    pass_on(0)
-    for copy in y_copies:
-        copy.wait()
-
-    def quad(i, carry):
-        for part in range(HALVES):
-            total = y_from[y, part, i].astype(jnp.float32)
-            for s in range(RING - 1):
-                total += y_buf[s, part, i].astype(jnp.float32)
-            z_own[i * HALVES + part] = total
-        return carry
-
-    lax.fori_loop(0, RING, quad, 0)
+
+    for k in range(NODES):
+        for s in range(1, RING):
+            y_copy(k, s).start()
+
+    def y_sum(k):
+        part, at = targets[k] % HALVES, targets[k] // HALVES
+        total = y_from[y, part, at].astype(jnp.float32)
+        for s in range(1, RING):
+            y_copy(k, s).wait_recv()
+            total += y_buf[s - 1, part, at].astype(jnp.float32)
+        z_own[targets[k]] = total
 
     def mine(step):
         return z_own[(node + step + NODES) % NODES]
@@ -475,19 +478,29 @@
             ring_copy(step, way).start()
 
     last = NODES // 2 - 1
+    y_sum(0)
     ring_step(0)
+    arrive(1)
+    pass_on(0)
+    y_sum(1)
+    y_sum(2)
+    ring_step(1)
     arrive(2)
-    ring_step(1)
+    y_sum(3)
+    y_sum(4)
+    ring_step(2)
     pass_on(1)
     pass_on(2)
-    ring_step(2)
     arrive(3)
+    y_sum(5)
+    y_sum(6)
+    ring_step(3)
     pass_on(3)
     pass_on(4)
-    ring_step(3)
     opposite()
     pass_on(5)
     pass_on(6)
+    y_sum(7)
     for way in range(2):
         ring_copy(last, way).wait_recv()
     grads = mine(0) + z_buf[0, last].astype(jnp.float32) + z_buf[1, last].astype(jnp.float32)
@@ -615,6 +628,9 @@
     for step in range(last + 1):
         for way in range(2):
             ring_copy(step, way).wait_send()
+    for k in range(NODES):
+        for s in range(1, RING):
+            y_copy(k, s).wait_send()
     in_left()
     up_left()
     out_left()
@@ -673,7 +689,7 @@
         + [dma((hosts,))] * 6
         + ([dma((NODES,))] * 2 + [dma((NODES, RING - 1))] * 2 + [dma((NODES, RING))] * 2) * 2
         + [dma] * 2
-        + [dma((RING - 1,))] * 2
+        + [dma((NODES, RING - 1))] * 2
         + [dma((2, NODES // 2))] * 2
         + [dma((pieces,)), dma((experts,)), dma((experts,)), dma((pieces,))],
         compiler_params=pltpu.CompilerParams(

time: 195 us -> 178 us (0.913)
  the two profiles are of different devices: /device:TPU:2 before, /device:TPU:24 now
where the time goes in v6:
time: 178 us; the launch traced here: 176 us
  Pallas kernels  166 us (93%)
  local copies, waits for them, and re-layouts  8.14 us (5%)
    pallas_call x1, Pallas kernels, layer(): pl.pallas_call(functools.partial(layer_kernel, experts), out_shape=[jax.S...  166 us
    unnamed x27, local copies, waits for them, and re-layouts  8.14 us

profile of v6, /device:TPU:24, one launch (start us, length us, event | category | flops | bytes accessed | tf_op | source)
XLA Modules:
  0.0 175.7 jit_solution(8083249811473834900)
XLA Ops:
  0.6 0.0 copy-start.8
  0.6 0.0 copy-start.9
  0.7 0.6 copy-done.8
  1.3 0.0 copy-done.9
  1.3 0.2 select_reduce_fusion.2
  1.5 0.0 copy-start.6
  1.5 0.7 copy-done.6
  2.1 0.0 copy-start.5
  2.1 0.1 fusion.2
  2.2 0.0 copy-start.4
  2.2 0.2 reduce_window_sum.11
  2.4 0.0 copy-start.7
  2.4 0.0 copy-start.2
  2.4 0.2 select_reduce_fusion.1
  2.6 0.0 copy-start.3
  2.7 0.1 fusion.pick_ref
  2.8 0.3 copy-done.7
  3.1 0.1 copy.18.gates_ref
  3.2 0.0 copy-done.5
  3.2 0.0 copy-done.4
  3.2 0.2 copy-done.2
  3.4 0.2 copy-done.3
  3.6 0.0 copy-start
  3.6 1.0 copy-done
  4.6 0.0 copy-start.1
  4.6 1.0 copy-done.1
  5.6 166.1 %layer.1 = (bf16[128,2048]{1,0:T(8,128)(2,1)S(1)}, f32[128,1]{1,0:T(8,128)S(1)}, f32[64,384]{1,0:T(8,128)S(1)}, f32[64,384]{1,0:T(8,128)S(1)}, f32[64,384]{1,0:T(8,128)S(1)}, /*index=5*/f32[64,384]{1,0:T(8,128)S(1)}) custom-call(bf16[160,128]{1,0:T(8,128)(2,1)S(1)} %fusion.1.place_ref, bf16[128,160]{1,0:T(8,128)(2,1)S(1)} %fusion.pick_ref, ...), custom_call_target="tpu_custom_call" | custom-call | tf_op jit(solution)/shard_map/layer/pallas_call | solution.py:656
  171.7 0.6 copy.19
  172.3 0.8 copy.25
  173.1 0.6 copy.26
  173.7 0.6 copy.27
  174.4 0.6 copy.28
  175.0 0.6 copy.29
  (2 shorter events, 0.0 us)
Async XLA Ops:
  0.6 0.7 copy-start.8
  0.6 0.7 copy-start.9
  1.5 0.7 copy-start.6
  2.1 1.0 copy-start.5
  2.2 1.0 copy-start.4
  2.4 0.7 copy-start.7
  2.4 0.9 copy-start.2
  2.6 0.9 copy-start.3
  3.6 1.0 copy-start
  4.6 1.0 copy-start.1

commit v7 on v6

--- a/solution.py
+++ b/solution.py
@@ -361,9 +361,9 @@
         )
 
     arrive(1)
-    up_there, up_left = exchange(hosts, dp, ex, up_from, up_to, up_send, up_recv)
     pass_on(0)
     arrive(2)
+    up_there, up_left = exchange(hosts, dp, ex, up_from, up_to, up_send, up_recv)
     pass_on(1)
     pass_on(2)
     in_there()
@@ -389,7 +389,6 @@
     to_rows(up_to, rows_up)
     multiply(7)
     own, _, begin_across, arrive, opposite, pass_on, complete = down
-    begin_across()
     own.start()
     hidden[...] = (silu_value(both[:, :ff]) * both[:, ff:]).astype(hidden.dtype)
 
@@ -432,6 +431,7 @@
     for k in range(NODES):
         for s in range(1, RING):
             y_copy(k, s).start()
+    begin_across()
 
     def y_sum(k):
         part, at = targets[k] % HALVES, targets[k] // HALVES
@@ -528,11 +528,16 @@
             state.at[q], spread.at[ex], s_send.at[q], s_recv.at[ex], (dp, middle(q, core))
         )
 
-    for q in range(pieces):
+    def spread_start(step, carry):
+        q = (ex + step) % pieces
 
         @pl.when(middle(q, core) != ex)
-        def _(q=q):
+        def _():
             spread_copy(q).start()
+
+        return carry
+
+    lax.fori_loop(0, pieces, spread_start, 0)
 
     def order_copy(step):
         target = (ex + step) % experts

time: 178 us -> 186 us (1.045)
  Pallas kernels: 166 us -> 173 us
    pallas_call x1, Pallas kernels: 166 us -> 173 us  [layer(): pl.pallas_call(functools.partial(layer_kernel, experts), out_shape=[jax.S...]
where the time goes in v7:
time: 186 us; the launch traced here: 183 us
  Pallas kernels  173 us (93%)
  local copies, waits for them, and re-layouts  8.14 us (4%)
    pallas_call x1, Pallas kernels, layer(): pl.pallas_call(functools.partial(layer_kernel, experts), out_shape=[jax.S...  173 us
    unnamed x27, local copies, waits for them, and re-layouts  8.14 us

profile of v7, /device:TPU:24, one launch (start us, length us, event | category | flops | bytes accessed | tf_op | source)
XLA Modules:
  0.0 182.6 jit_solution(16724272875828503168)
XLA Ops:
  0.6 0.0 copy-start.8
  0.6 0.0 copy-start.9
  0.7 0.6 copy-done.8
  1.3 0.0 copy-done.9
  1.3 0.2 select_reduce_fusion.2
  1.5 0.0 copy-start.6
  1.5 0.7 copy-done.6
  2.1 0.0 copy-start.5
  2.1 0.1 fusion.2
  2.2 0.0 copy-start.4
  2.2 0.2 reduce_window_sum.11
  2.4 0.0 copy-start.7
  2.4 0.0 copy-start.2
  2.4 0.2 select_reduce_fusion.1
  2.6 0.0 copy-start.3
  2.7 0.1 fusion.pick_ref
  2.8 0.3 copy-done.7
  3.1 0.1 copy.18.gates_ref
  3.2 0.0 copy-done.5
  3.2 0.0 copy-done.4
  3.2 0.2 copy-done.2
  3.4 0.2 copy-done.3
  3.6 0.0 copy-start
  3.6 1.0 copy-done
  4.6 0.0 copy-start.1
  4.6 1.0 copy-done.1
  5.6 173.0 %layer.1 = (bf16[128,2048]{1,0:T(8,128)(2,1)S(1)}, f32[128,1]{1,0:T(8,128)S(1)}, f32[64,384]{1,0:T(8,128)S(1)}, f32[64,384]{1,0:T(8,128)S(1)}, f32[64,384]{1,0:T(8,128)S(1)}, /*index=5*/f32[64,384]{1,0:T(8,128)S(1)}) custom-call(bf16[160,128]{1,0:T(8,128)(2,1)S(1)} %fusion.1.place_ref, bf16[128,160]{1,0:T(8,128)(2,1)S(1)} %fusion.pick_ref, ...), custom_call_target="tpu_custom_call" | custom-call | tf_op jit(solution)/shard_map/layer/pallas_call | solution.py:661
  178.7 0.6 copy.19
  179.2 0.8 copy.25
  180.0 0.6 copy.26
  180.7 0.6 copy.27
  181.3 0.6 copy.28
  182.0 0.6 copy.29
  (2 shorter events, 0.0 us)
Async XLA Ops:
  0.6 0.7 copy-start.8
  0.6 0.7 copy-start.9
  1.5 0.7 copy-start.6
  2.1 1.0 copy-start.5
  2.2 1.0 copy-start.4
  2.4 0.7 copy-start.7
  2.4 0.9 copy-start.2
  2.6 0.9 copy-start.3
  3.6 1.0 copy-start
  4.6 1.0 copy-start.1
